TPU v7x, 128 devices: a whole 4x4x4 slice. The times are simulated.
128 devices in a mesh: dp: 8 (over x, y_lo), tp: 16 (over z, y_hi, core).
Axes of the slice: x: 4, y: 4 (y_hi: 2, y_lo: 2; y = y_hi * 2 + y_lo), z: 4, core: 2. Of those that a mesh axis runs over, the one named last changes fastest.
Arguments:
- queries: bfloat16 [1024, 128, 576], P(('dp', 'tp')), may hold values from -48 to 48
- kv_cache: bfloat16 [1024, 1024, 576], P(('dp', 'tp')), may hold values from -6 to 6
- lengths: int32 [8, 16, 8], P(None, 'tp'), may hold values from 1 to 1024
- dest_group: int32 [8, 16], P(None, 'tp'), may hold values from 0 to 7, as said below
- moved_slot: int32 [8, 16], P(None, 'tp'), may hold values from 0 to 7
- residual_in: bfloat16 [1024, 7168], P('dp', 'tp'), may hold values from -31 to 31
- norm_gain: bfloat16 [7168], P('tp'), may hold values from 0.099609375 to 1.8984375
- up_value: bfloat16 [128, 512, 128], P('dp'), may hold values from -0.75 to 0.75
- out_proj: bfloat16 [16384, 7168], P('dp', 'tp'), may hold values from -0.046875 to 0.046875
- gate_proj: bfloat16 [7168, 18432], P('tp', 'dp'), may hold values from -0.0625 to 0.0625
- up_proj: bfloat16 [7168, 18432], P('tp', 'dp'), may hold values from -0.0625 to 0.0625
- down_proj: bfloat16 [18432, 7168], P('dp', 'tp'), may hold values from -0.046875 to 0.046875
Outputs:
- attended: bfloat16 [1024, 7168], P('dp', 'tp')
- layer_out: bfloat16 [1024, 7168], P('dp', 'tp')
Inputs may be any that keep to these rules, and one draw needn't show every extreme that they name: dest_group[g, t] = g XOR m_t, where the mask m_t lies in 1 to 7 and is the same for every g of column t; so dest_group[dest_group[g, t], t] = g.
All inputs are finite; a program needn't handle non-finite values.
Results may differ from a plain program's by a relative error of at most 0.022.
Values may be sent and summed in bfloat16 or wider, within the bound.
A program may use at most 128 MiB of HBM per device.

v0:
```python
import jax
import jax.numpy as jnp
from jax import lax
from jax.sharding import PartitionSpec as P

D = 7168
KV = 512


score_scale = 192.0 ** (-0.5)
norm_eps = 1e-06


def swapped_2(block, axis, distance):
    count = lax.axis_size(axis)
    route = []
    for low in range(count):
        high = low | 1 << distance
        if high != low and high < count:
            route += [(low, high), (high, low)]
    return lax.ppermute(block, axis, route)


def attend_block(query_rows, cache_rows, length_rows):
    scores = (
        jnp.einsum("rhc,rkc->rhk", query_rows, cache_rows, preferred_element_type=jnp.float32)
        * score_scale
    )
    position = lax.broadcasted_iota(jnp.int32, scores.shape, 2)
    allowed = position < length_rows[:, None, None]
    masked = jnp.where(allowed, scores, -jnp.inf)
    largest = jnp.max(masked, axis=2, keepdims=True)
    expterm = jnp.where(allowed, jnp.exp(masked - largest), 0.0)
    weights = (expterm / jnp.sum(expterm, axis=2, keepdims=True)).astype(jnp.bfloat16)
    latent = jnp.einsum(
        "rhk,rkc->rhc", weights, cache_rows[:, :, :KV], preferred_element_type=jnp.float32
    )
    return latent.astype(jnp.bfloat16)


def shards(
    queries,
    kv_cache,
    lengths,
    dest_group,
    moved_slot,
    residual_in,
    norm_gain,
    up_value,
    out_proj,
    gate_proj,
    up_proj,
    down_proj,
):
    group = lax.axis_index("dp")
    group_count = lax.axis_size("dp")
    bit_total = group_count.bit_length() - 1
    column_lengths = lengths[:, 0, :]
    own_lengths = lax.dynamic_index_in_dim(column_lengths, group, 0, keepdims=False)
    partner = lax.dynamic_index_in_dim(dest_group[:, 0], group, 0, keepdims=False)
    own_slot = lax.dynamic_index_in_dim(moved_slot[:, 0], group, 0, keepdims=False)
    partner_slot = lax.dynamic_index_in_dim(moved_slot[:, 0], partner, 0, keepdims=False)
    partner_lengths = lax.dynamic_index_in_dim(column_lengths, partner, 0, keepdims=False)
    incoming_length = lax.dynamic_index_in_dim(partner_lengths, partner_slot, 0, keepdims=False)
    swap_mask = jnp.bitwise_xor(partner, group)
    cache_len = kv_cache.shape[1]
    outgoing_cache = lax.dynamic_index_in_dim(kv_cache, own_slot, 0, keepdims=False)
    outgoing_query = lax.dynamic_index_in_dim(queries, own_slot, 0, keepdims=False)
    payload = jnp.concatenate((outgoing_cache, outgoing_query), axis=0)
    for bit_index in range(bit_total):
        swapped = swapped_2(payload, "dp", bit_index)
        payload = jnp.where(jnp.right_shift(swap_mask, bit_index) & 1 == 1, swapped, payload)
    cache_rows = lax.dynamic_update_index_in_dim(kv_cache, payload[:cache_len], own_slot, 0)
    query_rows = lax.dynamic_update_index_in_dim(queries, payload[cache_len:], own_slot, 0)
    slot_ids = jnp.arange(own_lengths.shape[0], dtype=jnp.int32)
    length_rows = jnp.where(slot_ids == own_slot, incoming_length, own_lengths)
    latent = attend_block(query_rows, cache_rows, length_rows)
    head_rows = lax.all_to_all(latent, "dp", split_axis=1, concat_axis=0, tiled=True)
    values = jnp.einsum(
        "rhc,hcd->rhd", head_rows, up_value, preferred_element_type=jnp.float32
    ).astype(jnp.bfloat16)
    values = values.reshape(values.shape[0], values.shape[1] * values.shape[2])
    head_terms = jnp.dot(
        lax.all_gather(values, "tp", axis=0, tiled=True),
        out_proj,
        preferred_element_type=jnp.float32,
    )
    attn = lax.psum_scatter(
        head_terms.astype(jnp.bfloat16), "dp", scatter_dimension=0, tiled=True
    ).astype(jnp.float32)
    resid = residual_in.astype(jnp.float32) + attn
    square_sum = lax.psum(jnp.sum(resid * resid, axis=1), "tp")
    row_scale = lax.rsqrt(square_sum / D + norm_eps)
    normed = (resid * row_scale[:, None] * norm_gain.astype(jnp.float32)).astype(jnp.bfloat16)
    block_rows = lax.all_gather(normed, "dp", axis=0, tiled=True)
    gate_part = jnp.dot(block_rows, gate_proj, preferred_element_type=jnp.float32)
    upward_part = jnp.dot(block_rows, up_proj, preferred_element_type=jnp.float32)
    partial_gate = jnp.concatenate((gate_part, upward_part), axis=1)
    ff_local = gate_proj.shape[1]
    summed = lax.psum(partial_gate.astype(jnp.bfloat16), "tp").astype(jnp.float32)
    hidden = (jax.nn.silu(summed[:, :ff_local]) * summed[:, ff_local:]).astype(jnp.bfloat16)
    block_rows = hidden
    down = lax.psum_scatter(
        jnp.dot(block_rows, down_proj, preferred_element_type=jnp.float32).astype(jnp.bfloat16),
        "dp",
        scatter_dimension=0,
        tiled=True,
    ).astype(jnp.float32)
    return (attn.astype(jnp.bfloat16), (resid + down).astype(jnp.bfloat16))


def solution(mesh):
    return jax.shard_map(
        shards,
        mesh=mesh,
        in_specs=(
            P(("dp", "tp"), None, None),
            P(("dp", "tp"), None, None),
            P(None, "tp", None),
            P(None, "tp"),
            P(None, "tp"),
            P("dp", "tp"),
            P("tp"),
            P("dp", None, None),
            P("dp", "tp"),
            P("tp", "dp"),
            P("tp", "dp"),
            P("dp", "tp"),
        ),
        out_specs=(P("dp", "tp"), P("dp", "tp")),
        check_vma=False,
    )
```

profile of v0, /device:TPU:3, one launch (start us, length us, event | category | flops | bytes accessed | tf_op | source)
XLA Modules:
  0.0 628.4 jit_solution(10987646806100762388)
XLA Ops:
  21.9 2.6 copy.29
  26.4 28.4 %collective-permute-done = bf16[1152,576]{0,1:T(8,128)(2,1)} collective-permute-done((bf16[1152,576]{0,1:T(8,128)(2,1)}, bf16[1152,576]{0,1:T(8,128)(2,1)}, u32[]{:S(2)}, u32[]{:S(2)}) %collective-permute-start) | collective-permute-done | bytes 1327136 | tf_op jit(solution)/shard_map/ppermute | solution.py:21
  54.8 2.6 copy.30
  57.4 2.9 broadcast_select_fusion
  62.9 29.7 %collective-permute-done.1 = bf16[1152,576]{0,1:T(8,128)(2,1)S(1)} collective-permute-done((bf16[1152,576]{0,1:T(8,128)(2,1)}, bf16[1152,576]{0,1:T(8,128)(2,1)S(1)}, u32[]{:S(2)}, u32[]{:S(2)}) %collective-permute-start.1) | collective-permute-done | bytes 1327136 | tf_op jit(solution)/shard_map/ppermute | solution.py:21
  94.3 2.7 broadcast_select_fusion.1
  97.0 2.6 copy.33
  102.8 14.1 %copy.36 = bf16[8,1024,576]{2,1,0:T(8,128)(2,1)} copy(bf16[8,1024,576]{1,2,0:T(8,128)(2,1)} %param.13) | data formatting | bytes 18874368 | tf_op args[1]
  120.6 9.3 %collective-permute-done.2 = bf16[1152,576]{0,1:T(8,128)(2,1)S(1)} collective-permute-done((bf16[1152,576]{0,1:T(8,128)(2,1)}, bf16[1152,576]{0,1:T(8,128)(2,1)S(1)}, u32[]{:S(2)}, u32[]{:S(2)}) %collective-permute-start.2) | collective-permute-done | bytes 1327136 | tf_op jit(solution)/shard_map/ppermute | solution.py:21
  138.6 9.5 %fusion.25 = (f32[8,128]{1,0:T(8,128)S(1)}, f32[8,128,1024]{2,1,0:T(8,128)}) fusion(s32[8]{0:T(128)S(1)} %compare_select_fusion, bf16[8,128,576]{1,2,0:T(8,128)(2,1)S(1)} %constant_dynamic-update-slice_fusion, bf16[8,1024,576]{2,1,0:T(8,128)(2,1)} %fusion.17), kind=kOutput, calls=%fused_computation.51 | convolution fusion | flops 1215300608 | bytes 14815264 | tf_op jit(solution)/shard_map/sub | solution.py:33
  148.1 6.2 fusion.11
  154.8 15.7 %all_to_all.18 = bf16[8,128,512]{2,0,1:T(8,128)(2,1)S(1)} all-to-all(bf16[8,128,512]{2,0,1:T(8,128)(2,1)S(1)} %copy.38), channel_id=1, replica_groups=mesh['dp'=8,'tp'=16] {'dp'}, dimensions={1} | all-to-all | bytes 2097152 | tf_op jit(solution)/shard_map/all_to_all | solution.py:78
  172.1 61.0 %all-gather.2.cloned.1.call-done = bf16[1024,2048]{1,0:T(8,128)(2,1)} async-done(((bf16[64,2048]{1,0:T(8,128)(2,1)}), bf16[1024,2048]{1,0:T(8,128)(2,1)}) %all-gather.2.cloned.1.call-update) | async-done | bytes 4194320 | tf_op jit(solution)/shard_map/all_gather | solution.py:84
  233.1 4.9 convolution_convert_fusion.2
  239.4 31.2 %reduce-scatter.7.cloned.1.call-done = bf16[128,448]{1,0:T(8,128)(2,1)} async-done(((bf16[1024,448]{1,0:T(8,128)(2,1)}), bf16[128,448]{1,0:T(8,128)(2,1)}) %reduce-scatter.7.cloned.1.call-update) | async-done | bytes 114704
  271.8 37.0 %psum.14 = f32[128]{0:T(128)S(1)} all-reduce(f32[128]{0:T(128)S(1)} %multiply_reduce_fusion), channel_id=1, replica_groups=mesh['dp'=8,'tp'=16] {'tp'}, use_global_device_ids=true, to_apply=%region_4.5 | all-reduce | flops 128 | bytes 1024 | tf_op jit(solution)/shard_map/psum | solution.py:92
  308.9 24.6 %all_gather.7 = bf16[1024,448]{0,1:T(8,128)(2,1)S(1)} all-gather(bf16[128,448]{0,1:T(8,128)(2,1)S(1)} %multiply_convert_fusion), channel_id=1, replica_groups=mesh['dp'=8,'tp'=16] {'dp'}, dimensions={0}, use_global_device_ids=true | all-gather | bytes 1032192 | tf_op jit(solution)/shard_map/all_gather | solution.py:95
  333.5 4.6 convolution_convert_fusion
  338.1 2.9 convolution_convert_fusion.1
  341.0 4.7 pad_maximum_fusion
  345.8 216.4 %all-reduce.2.cloned.1.call-done = bf16[1024,4608]{1,0:T(8,128)(2,1)} async-done(((bf16[1024,4608]{1,0:T(8,128)(2,1)}), bf16[1024,4608]{1,0:T(8,128)(2,1)}) %all-reduce.2.cloned.1.call-update) | async-done | bytes 9437200 | tf_op jit(solution)/shard_map/psum | solution.py:100
  562.3 12.8 %convert_element_type.53 = f32[1024,4608]{1,0:T(8,128)} convert(bf16[1024,4608]{1,0:T(8,128)(2,1)} %all-reduce.2.cloned.1.call-done) | non-fusion elementwise | flops 4718592 | bytes 28311552 | tf_op jit(solution)/shard_map/convert_element_type | solution.py:100
  575.1 10.2 %fusion.14 = bf16[1024,448]{0,1:T(8,128)(2,1)S(1)} fusion(bf16[2304,448]{0,1:T(8,128)(2,1)} %param.23, f32[1024,4608]{1,0:T(8,128)} %convert_element_type.53), kind=kOutput, calls=%fused_computation.23 | convolution fusion | flops 2128543744 | bytes 21856256 | tf_op jit(solution)/shard_map/dot_general | solution.py:104
  586.6 33.5 %reduce-scatter.9.cloned.1.call-done = bf16[128,448]{1,0:T(8,128)(2,1)} async-done(((bf16[1024,448]{1,0:T(8,128)(2,1)}), bf16[128,448]{1,0:T(8,128)(2,1)}) %reduce-scatter.9.cloned.1.call-update) | async-done | bytes 114704
  (59 shorter events, 38.0 us)
Async XLA Ops:
  7.2 163.4 %copy-start = (bf16[16,512,128]{2,1,0:T(8,128)(2,1)S(1)}, bf16[16,512,128]{2,1,0:T(8,128)(2,1)}, u32[]{:S(2)}) copy-start(bf16[16,512,128]{2,1,0:T(8,128)(2,1)} %param.19) | copy-start | bytes 6291460
  7.2 225.9 %all-gather.2.cloned.1.call-start = ((), (), s32[]{:S(2)}) async-start(), calls=%async_computation.3 | async-start | bytes 4456448 | tf_op jit(solution)/shard_map/all_gather | solution.py:84
  8.6 7.0 %copy-start.4 = (bf16[8,128,576]{1,2,0:T(8,128)(2,1)}, bf16[8,128,576]{1,2,0:T(8,128)(2,1)S(1)}, u32[]{:S(2)}) copy-start(bf16[8,128,576]{1,2,0:T(8,128)(2,1)S(1)} %copy.57) | copy-start | bytes 3538948
  24.5 30.3 %collective-permute-start = (bf16[1152,576]{0,1:T(8,128)(2,1)}, bf16[1152,576]{0,1:T(8,128)(2,1)}, u32[]{:S(2)}, u32[]{:S(2)}) collective-permute-start(bf16[1152,576]{0,1:T(8,128)(2,1)} %copy.29), channel_id=1, source_target_pairs={{0,16},{16,0},{32,48},{48,32},{64,80},{80,64},{96,112},{112,96},{1... | collective-permute-start | bytes 3981320 | tf_op jit(solution)/shard_map/ppermute | solution.py:21
  62.9 29.7 %collective-permute-start.1 = (bf16[1152,576]{0,1:T(8,128)(2,1)}, bf16[1152,576]{0,1:T(8,128)(2,1)S(1)}, u32[]{:S(2)}, u32[]{:S(2)}) collective-permute-start(bf16[1152,576]{0,1:T(8,128)(2,1)} %copy.31), channel_id=1, source_target_pairs={{0,32},{32,0},{16,48},{48,16},{64,96},{96,64},{80,112},{112,80},{1... | collective-permute-start | bytes 3981320 | tf_op jit(solution)/shard_map/ppermute | solution.py:21
  99.6 30.3 %collective-permute-start.2 = (bf16[1152,576]{0,1:T(8,128)(2,1)}, bf16[1152,576]{0,1:T(8,128)(2,1)S(1)}, u32[]{:S(2)}, u32[]{:S(2)}) collective-permute-start(bf16[1152,576]{0,1:T(8,128)(2,1)} %copy.33), channel_id=1, source_target_pairs={{0,64},{64,0},{16,80},{80,16},{32,96},{96,32},{48,112},{112,48},{1... | collective-permute-start | bytes 3981320 | tf_op jit(solution)/shard_map/ppermute | solution.py:21
  131.6 3.6 copy-start.5
  133.2 1.1 copy-start.2
  171.8 98.8 %reduce-scatter.7.cloned.1.call-start = ((), (), s32[]{:S(2)}) async-start(), calls=%async_computation.5 | async-start | bytes 1179648
  238.0 1.4 copy-start.7
  238.0 33.7 %copy-start.6 = (bf16[128,448]{0,1:T(8,128)(2,1)S(1)}, bf16[128,448]{0,1:T(8,128)(2,1)}, u32[]{:S(2)}) copy-start(bf16[128,448]{0,1:T(8,128)(2,1)} %param.17) | copy-start | bytes 344068
  239.3 322.9 %all-reduce.2.cloned.1.call-start = ((), (), s32[]{:S(2)}) async-start(), calls=%async_computation.4 | async-start | bytes 18874368 | tf_op jit(solution)/shard_map/psum | solution.py:100
  271.7 349.4 %copy-start.3 = (bf16[128,448]{0,1:T(8,128)(2,1)}, bf16[128,448]{0,1:T(8,128)(2,1)S(1)}, u32[]{:S(2)}) copy-start(bf16[128,448]{0,1:T(8,128)(2,1)S(1)} %copy.43) | copy-start | bytes 344068
  333.5 4.6 copy-start.8
  345.8 274.3 %reduce-scatter.9.cloned.1.call-start = ((), (), s32[]{:S(2)}) async-start(), calls=%async_computation.6 | async-start | bytes 1179648
  575.1 46.8 %copy-start.1 = (bf16[16,512,128]{2,1,0:T(8,128)(2,1)S(1)}, bf16[16,512,128]{2,1,0:T(8,128)(2,1)}, u32[]{:S(2)}) copy-start(bf16[16,512,128]{2,1,0:T(8,128)(2,1)} %param.19) | copy-start | bytes 6291460
Sparse Core Ops, SparseCore 0:
  172.0 61.0 all-gather.1
  239.5 31.1 reduce-scatter.6
  345.9 216.3 all-reduce.1
  586.7 33.3 reduce-scatter.8
where the time goes:
time: 634 us; the launch traced here: 628 us
  waiting for transfers between devices  410 us (65%)
  blocking collectives  77.3 us (12%)
  local copies, waits for them, and re-layouts  49.3 us (8%)
  matrix products  38.7 us (6%)
  other arithmetic  29.7 us (5%)
  between operations  20.2 us (3%)
    psum x1, waiting for transfers between devices, shards(): lax.psum(partial_gate.astype(jnp.bfloat16), 'tp').astype(jnp.float32)  216 us
    ppermute x3, waiting for transfers between devices, swapped_2(): return lax.ppermute(block, axis, route)  67.4 us
    unnamed x6, waiting for transfers between devices  64.8 us
    all_gather x1, waiting for transfers between devices, shards(): lax.all_gather(values, 'tp', axis=0, tiled=True)  61 us
    psum x1, blocking collectives, shards(): square_sum = lax.psum(jnp.sum(resid * resid, axis=1), 'tp')  37 us
    all_gather x1, blocking collectives, shards(): block_rows = lax.all_gather(normed, 'dp', axis=0, tiled=True)  24.6 us
    unnamed x24, local copies, waits for them, and re-layouts  21.3 us
    all_to_all x1, blocking collectives, shards(): lax.all_to_all(latent, 'dp', split_axis=1, concat_axis=0, tiled=True)  15.7 us
  transfers between devices with their start and end apart: 7, of which 7 were waited for; matrix products, arithmetic and copies ran while one was open for 3% of the time, Pallas kernels for 0%

commit v1 on v0

v1 whole, which is shorter than its diff:
```python
import jax
import jax.numpy as jnp
from jax import lax
from jax.sharding import PartitionSpec as P

D = 7168
KV = 512


score_scale = 192.0 ** (-0.5)
norm_eps = 1e-06


def attend_block(query_rows, cache_rows, length_rows):
    scores = (
        jnp.einsum("rhc,rkc->rhk", query_rows, cache_rows, preferred_element_type=jnp.float32)
        * score_scale
    )
    position = lax.broadcasted_iota(jnp.int32, scores.shape, 2)
    allowed = position < length_rows[:, None, None]
    masked = jnp.where(allowed, scores, -jnp.inf)
    largest = jnp.max(masked, axis=2, keepdims=True)
    expterm = jnp.where(allowed, jnp.exp(masked - largest), 0.0)
    weights = (expterm / jnp.sum(expterm, axis=2, keepdims=True)).astype(jnp.bfloat16)
    latent = jnp.einsum(
        "rhk,rkc->rhc", weights, cache_rows[:, :, :KV], preferred_element_type=jnp.float32
    )
    return latent.astype(jnp.bfloat16)


def placed_sources(partners, slots, slot_count):
    groups = jnp.arange(partners.shape[0], dtype=jnp.int32)[:, None]
    slot_ids = jnp.arange(slot_count, dtype=jnp.int32)[None, :]
    incoming = partners[:, None] * slot_count + slots[partners][:, None]
    staying = groups * slot_count + slot_ids
    return jnp.where(slot_ids == slots[:, None], incoming, staying).reshape(-1)


def shards(
    queries,
    kv_cache,
    lengths,
    dest_group,
    moved_slot,
    residual_in,
    norm_gain,
    up_value,
    out_proj,
    gate_proj,
    up_proj,
    down_proj,
):
    group = lax.axis_index("dp")
    own_lengths = lax.dynamic_index_in_dim(lengths[:, 0, :], group, 0, keepdims=False)
    latent = attend_block(queries, kv_cache, own_lengths)
    head_rows = lax.all_to_all(latent, "dp", split_axis=1, concat_axis=0, tiled=True)
    values = jnp.einsum(
        "rhc,hcd->rhd", head_rows, up_value, preferred_element_type=jnp.float32
    ).astype(jnp.bfloat16)
    values = values.reshape(values.shape[0], values.shape[1] * values.shape[2])
    values = values[placed_sources(dest_group[:, 0], moved_slot[:, 0], own_lengths.shape[0])]
    head_terms = jnp.dot(
        lax.all_gather(values, "tp", axis=0, tiled=True),
        out_proj,
        preferred_element_type=jnp.float32,
    )
    attn = lax.psum_scatter(
        head_terms.astype(jnp.bfloat16), "dp", scatter_dimension=0, tiled=True
    ).astype(jnp.float32)
    resid = residual_in.astype(jnp.float32) + attn
    square_sum = jnp.sum(resid * resid, axis=1)
    scaled = (resid * norm_gain.astype(jnp.float32)).astype(jnp.bfloat16)
    block_rows = lax.all_gather(scaled, "dp", axis=0, tiled=True)
    block_sums = lax.all_gather(square_sum, "dp", axis=0, tiled=True)
    gate_part = jnp.dot(block_rows, gate_proj, preferred_element_type=jnp.float32)
    upward_part = jnp.dot(block_rows, up_proj, preferred_element_type=jnp.float32)
    partial_gate = jnp.concatenate((gate_part, upward_part), axis=1)
    ff_local = gate_proj.shape[1]
    summed = lax.psum_scatter(
        partial_gate.astype(jnp.bfloat16), "tp", scatter_dimension=0, tiled=True
    ).astype(jnp.float32)
    row_sums = lax.psum_scatter(block_sums, "tp", scatter_dimension=0, tiled=True)
    row_scale = lax.rsqrt(row_sums / D + norm_eps)[:, None]
    summed = summed * row_scale
    hidden = (jax.nn.silu(summed[:, :ff_local]) * summed[:, ff_local:]).astype(jnp.bfloat16)
    hidden = lax.all_gather(hidden, "tp", axis=0, tiled=True)
    block_rows = hidden
    down = lax.psum_scatter(
        jnp.dot(block_rows, down_proj, preferred_element_type=jnp.float32).astype(jnp.bfloat16),
        "dp",
        scatter_dimension=0,
        tiled=True,
    ).astype(jnp.float32)
    return (attn.astype(jnp.bfloat16), (resid + down).astype(jnp.bfloat16))


def solution(mesh):
    return jax.shard_map(
        shards,
        mesh=mesh,
        in_specs=(
            P(("dp", "tp"), None, None),
            P(("dp", "tp"), None, None),
            P(None, "tp", None),
            P(None, "tp"),
            P(None, "tp"),
            P("dp", "tp"),
            P("tp"),
            P("dp", None, None),
            P("dp", "tp"),
            P("tp", "dp"),
            P("tp", "dp"),
            P("dp", "tp"),
        ),
        out_specs=(P("dp", "tp"), P("dp", "tp")),
        check_vma=False,
    )
```

time: 634 us -> 408 us (0.64)
  waiting for transfers between devices: 410 us -> 247 us
  local copies, waits for them, and re-layouts: 49.3 us -> 10.5 us
  other arithmetic: 29.7 us -> 7.85 us
    psum x1 -> x0, waiting for transfers between devices: 216 us -> none  [shards(): lax.psum(partial_gate.astype(jnp.bfloat16), 'tp').astype(jnp.float32)]
    ppermute x3 -> x0, waiting for transfers between devices: 67.4 us -> none  [swapped_2(): return lax.ppermute(block, axis, route)]
    all_gather x0 -> x1, waiting for transfers between devices: none -> 58.3 us  [shards(): hidden = lax.all_gather(hidden, 'tp', axis=0, tiled=True)]
    reduce_scatter x0 -> x1, waiting for transfers between devices: none -> 56.2 us  [shards(): lax.psum_scatter(partial_gate.astype(jnp.bfloat16), 'tp', scatter_dimensi...]
    unnamed x0 -> x1, blocking collectives: none -> 46.4 us
    psum x1 -> x0, blocking collectives: 37 us -> none  [shards(): square_sum = lax.psum(jnp.sum(resid * resid, axis=1), 'tp')]
    all_to_all x1 -> x0, blocking collectives: 15.7 us -> none  [shards(): lax.all_to_all(latent, 'dp', split_axis=1, concat_axis=0, tiled=True)]
    unnamed x24 -> x21, local copies, waits for them, and re-layouts: 21.3 us -> 5.9 us
  transfers between devices with their start and end apart: 7 -> 6, of which waited for: 7 -> 6; matrix products, arithmetic and copies ran while one was open for 3% -> 0% of each run, Pallas kernels for 0% -> 0%
where the time goes in v1:
time: 408 us; the launch traced here: 402 us
  waiting for transfers between devices  247 us (61%)
  blocking collectives  81.4 us (20%)
  matrix products  34.6 us (8%)
  between operations  14.6 us (4%)
  local copies, waits for them, and re-layouts  10.5 us (3%)
  other arithmetic  7.85 us (2%)
  starting transfers between devices  5.45 us (1%)
    unnamed x7, waiting for transfers between devices  61.9 us
    all_gather x1, waiting for transfers between devices, shards(): hidden = lax.all_gather(hidden, 'tp', axis=0, tiled=True)  58.3 us
    all_gather x1, waiting for transfers between devices, shards(): lax.all_gather(values, 'tp', axis=0, tiled=True)  57.8 us
    reduce_scatter x1, waiting for transfers between devices, shards(): lax.psum_scatter(partial_gate.astype(jnp.bfloat16), 'tp', scatter_dimensi...  56.2 us
    unnamed x1, blocking collectives  46.4 us
    all_gather x1, blocking collectives, shards(): block_rows = lax.all_gather(scaled, 'dp', axis=0, tiled=True)  23.1 us
    all_to_all x1, waiting for transfers between devices, shards(): lax.all_to_all(latent, 'dp', split_axis=1, concat_axis=0, tiled=True)  13.1 us
    all_gather x1, blocking collectives, shards(): block_sums = lax.all_gather(square_sum, 'dp', axis=0, tiled=True)  11.9 us
  transfers between devices with their start and end apart: 6, of which 6 were waited for; matrix products, arithmetic and copies ran while one was open for 0% of the time, Pallas kernels for 0%

profile of v1, /device:TPU:3, one launch (start us, length us, event | category | flops | bytes accessed | tf_op | source)
XLA Modules:
  0.0 401.6 jit_solution(9177672814307021503)
XLA Ops:
  8.0 8.8 %fusion.22 = (f32[8,128]{1,0:T(8,128)S(1)}, f32[8,128,1024]{2,1,0:T(8,128)}) fusion(s32[8]{0:T(128)S(1)} %dynamic-slice_bitcast_fusion, bf16[8,128,576]{1,2,0:T(8,128)(2,1)} %param.12, bf16[8,1024,576]{1,2,0:T(8,128)(2,1)} %param.13), kind=kOutput, calls=%fused_computation.49 | convolution fusion | flops 1215300608 | bytes 14815264 | tf_op jit(solution)/shard_map/sub | solution.py:23
  16.8 7.6 %fusion.8 = bf16[8,128,512]{2,1,0:T(8,128)(2,1)S(1)} fusion(bf16[8,1024,576]{1,2,0:T(8,128)(2,1)} %param.13, f32[8,128,1024]{2,1,0:T(8,128)} %get-tuple-element.5, f32[8,128]{1,0:T(8,128)S(1)} %get-tuple-element.4), kind=kOutput, calls=%fused_computation.17 | convolution fusion | flops 1076363264 | bytes 13635584 | tf_op jit(solution)/shard_map/rhk,rkc->rhc/dot_general | solution.py:25
  24.4 1.6 copy.20
  26.0 5.3 %all-to-all-start = ((bf16[8,128,512]{2,0,1:T(8,128)(2,1)}), bf16[8,128,512]{2,0,1:T(8,128)(2,1)S(1)}, u32[]{:S(2)}, u32[]{:S(2)}) async-start(bf16[8,128,512]{2,0,1:T(8,128)(2,1)} %copy.20), calls=%async_computation | async-start | bytes 2097152 | tf_op jit(solution)/shard_map/all_to_all | solution.py:56
  32.1 13.1 %all-to-all-done = bf16[8,128,512]{2,0,1:T(8,128)(2,1)S(1)} async-done(((bf16[8,128,512]{2,0,1:T(8,128)(2,1)}), bf16[8,128,512]{2,0,1:T(8,128)(2,1)S(1)}, u32[]{:S(2)}, u32[]{:S(2)}) %all-to-all-start) | async-done | bytes 1048608 | tf_op jit(solution)/shard_map/all_to_all | solution.py:56
  45.7 1.5 gather_fusion.1
  47.3 57.8 %all-gather.7.cloned.1.call-done = bf16[1024,2048]{1,0:T(8,128)(2,1)} async-done(((bf16[64,2048]{1,0:T(8,128)(2,1)}), bf16[1024,2048]{1,0:T(8,128)(2,1)}) %all-gather.7.cloned.1.call-update) | async-done | bytes 4194320 | tf_op jit(solution)/shard_map/all_gather | solution.py:63
  105.1 4.9 %convolution_convert_fusion.3 = bf16[1024,448]{0,1:T(8,128)(2,1)S(1)} fusion(bf16[1024,2048]{1,0:T(8,128)(2,1)} %all-gather.7.cloned.1.call-done, bf16[2048,448]{0,1:T(8,128)(2,1)} %param.20), kind=kOutput, calls=%fused_computation.19 | convolution fusion | flops 1879506944 | bytes 6946816 | tf_op jit(solution)/shard_map/dot_general | solution.py:62
  109.9 1.3 copy.23
  111.3 30.9 %reduce-scatter.10.cloned.1.call-done = bf16[128,448]{1,0:T(8,128)(2,1)} async-done(((bf16[1024,448]{1,0:T(8,128)(2,1)}), bf16[128,448]{1,0:T(8,128)(2,1)}) %reduce-scatter.10.cloned.1.call-update) | async-done | bytes 114704
  142.2 1.0 copy.24
  143.4 23.1 %all_gather.13 = bf16[1024,448]{0,1:T(8,128)(2,1)S(1)} all-gather(bf16[128,448]{0,1:T(8,128)(2,1)S(1)} %get-tuple-element.3), channel_id=1, replica_groups=mesh['dp'=8,'tp'=16] {'dp'}, dimensions={0}, use_global_device_ids=true | all-gather | bytes 1032192 | tf_op jit(solution)/shard_map/all_gather | solution.py:73
  166.5 4.6 %convolution_convert_fusion = bf16[1024,2304]{1,0:T(8,128)(2,1)S(1)} fusion(bf16[1024,448]{0,1:T(8,128)(2,1)S(1)} %all_gather.13, bf16[448,2304]{1,0:T(8,128)(2,1)} %param.22), kind=kOutput, calls=%fused_computation.6 | convolution fusion | flops 2116288512 | bytes 7700480 | tf_op jit(solution)/shard_map/dot_general | solution.py:76
  171.1 2.9 convolution_convert_fusion.1
  174.1 4.7 %pad_maximum_fusion = bf16[1024,4608]{1,0:T(8,128)(2,1)} fusion(bf16[1024,2304]{1,0:T(8,128)(2,1)S(1)} %convolution_convert_fusion, bf16[1024,2304]{1,0:T(8,128)(2,1)S(1)} %convolution_convert_fusion.1), kind=kLoop, calls=%fused_computation.3 | loop fusion | flops 18874368 | bytes 18874368 | tf_op jit(solution)/shard_map/concatenate | solution.py:77
  180.7 11.9 %all-gather.1 = f32[8,1,128]{2,1,0:T(1,128)S(1)} all-gather(f32[1,1,128]{2,1,0:T(1,128)S(1)} %bitcast.48), channel_id=1, replica_groups=mesh['dp'=8,'tp'=16] {'dp'}, dimensions={0}, use_global_device_ids=true | all-gather | bytes 4608 | tf_op jit(solution)/shard_map/all_gather | solution.py:74
  192.6 46.4 %all-reduce = f32[1024]{0:T(1024)S(1)} all-reduce(f32[1024]{0:T(1024)S(1)} %bitcast.47), channel_id=5, replica_groups=mesh['dp'=8,'tp'=16] {'tp'}, use_global_device_ids=true, to_apply=%region_5.6.clone | all-reduce | flops 1024 | bytes 8192
  239.0 56.2 %reduce-scatter.8.cloned.1.call-done = bf16[64,4608]{1,0:T(8,128)(2,1)} async-done(((bf16[1024,4608]{1,0:T(8,128)(2,1)}), bf16[64,4608]{1,0:T(8,128)(2,1)}) %reduce-scatter.8.cloned.1.call-update) | async-done | bytes 589840 | tf_op jit(solution)/shard_map/reduce_scatter | solution.py:79
  295.2 1.2 convert_multiply_fusion
  297.4 58.3 %all-gather.5.cloned.1.call-done = bf16[1024,2304]{1,0:T(8,128)(2,1)} async-done(((bf16[64,2304]{1,0:T(8,128)(2,1)}), bf16[1024,2304]{1,0:T(8,128)(2,1)}) %all-gather.5.cloned.1.call-update) | async-done | bytes 4718608 | tf_op jit(solution)/shard_map/all_gather | solution.py:86
  355.7 5.3 %convolution_convert_fusion.2 = bf16[1024,448]{0,1:T(8,128)(2,1)S(1)} fusion(bf16[1024,2304]{1,0:T(8,128)(2,1)} %all-gather.5.cloned.1.call-done, bf16[2304,448]{0,1:T(8,128)(2,1)} %param.23), kind=kOutput, calls=%fused_computation.18 | convolution fusion | flops 2114387968 | bytes 7700480 | tf_op jit(solution)/shard_map/dot_general | solution.py:89
  361.0 1.3 copy.25
  362.4 30.9 %reduce-scatter.12.cloned.1.call-done = bf16[128,448]{1,0:T(8,128)(2,1)} async-done(((bf16[1024,448]{1,0:T(8,128)(2,1)}), bf16[128,448]{1,0:T(8,128)(2,1)}) %reduce-scatter.12.cloned.1.call-update) | async-done | bytes 114704
  393.3 1.0 copy.26
  (44 shorter events, 5.4 us)
Async XLA Ops:
  7.2 38.0 %copy-start = (bf16[16,512,128]{2,1,0:T(8,128)(2,1)S(1)}, bf16[16,512,128]{2,1,0:T(8,128)(2,1)}, u32[]{:S(2)}) copy-start(bf16[16,512,128]{2,1,0:T(8,128)(2,1)} %param.19) | copy-start | bytes 6291460
  24.4 6.9 %copy-start.6 = (s32[8,1]{0,1:T(1,128)S(1)}, s32[8,1]{0,1:T(1,128)}, u32[]{:S(2)}) copy-start(s32[8,1]{0,1:T(1,128)} %param.15) | copy-start | bytes 100
  24.4 6.9 %copy-start.1 = (s32[8,1]{0,1:T(1,128)S(1)}, s32[8,1]{0,1:T(1,128)}, u32[]{:S(2)}) copy-start(s32[8,1]{0,1:T(1,128)} %param.16) | copy-start | bytes 100
  26.0 19.2 %all-to-all-start = ((bf16[8,128,512]{2,0,1:T(8,128)(2,1)}), bf16[8,128,512]{2,0,1:T(8,128)(2,1)S(1)}, u32[]{:S(2)}, u32[]{:S(2)}) async-start(bf16[8,128,512]{2,0,1:T(8,128)(2,1)} %copy.20), calls=%async_computation | async-start | bytes 2097152 | tf_op jit(solution)/shard_map/all_to_all | solution.py:56
  31.2 73.8 %all-gather.7.cloned.1.call-start = ((), (), s32[]{:S(2)}) async-start(), calls=%async_computation.6 | async-start | bytes 4456448 | tf_op jit(solution)/shard_map/all_gather | solution.py:63
  47.2 64.1 %copy-start.4 = (bf16[448]{0:T(512)(128)(2,1)S(1)}, bf16[448]{0:T(512)(128)(2,1)}, u32[]{:S(2)}) copy-start(bf16[448]{0:T(512)(128)(2,1)} %param.18) | copy-start | bytes 2692
  47.2 96.0 %copy-start.3 = (bf16[128,448]{0,1:T(8,128)(2,1)S(1)}, bf16[128,448]{0,1:T(8,128)(2,1)}, u32[]{:S(2)}) copy-start(bf16[128,448]{0,1:T(8,128)(2,1)} %param.17) | copy-start | bytes 344068
  47.2 95.0 %reduce-scatter.10.cloned.1.call-start = ((), (), s32[]{:S(2)}) async-start(), calls=%async_computation.7 | async-start | bytes 1179648
  111.3 184.0 %reduce-scatter.8.cloned.1.call-start = ((), (), s32[]{:S(2)}) async-start(), calls=%async_computation.4 | async-start | bytes 10027008 | tf_op jit(solution)/shard_map/reduce_scatter | solution.py:79
  143.3 251.1 %copy-start.2 = (bf16[128,448]{0,1:T(8,128)(2,1)}, bf16[128,448]{0,1:T(8,128)(2,1)S(1)}, u32[]{:S(2)}) copy-start(bf16[128,448]{0,1:T(8,128)(2,1)S(1)} %copy.24) | copy-start | bytes 344068
  166.5 4.6 %copy-start.5 = (bf16[448,2304]{1,0:T(8,128)(2,1)S(1)}, bf16[448,2304]{1,0:T(8,128)(2,1)}, u32[]{:S(2)}) copy-start(bf16[448,2304]{1,0:T(8,128)(2,1)} %param.21) | copy-start | bytes 6193156
  178.8 0.7 copy-start.7
  178.8 176.9 %all-gather.5.cloned.1.call-start = ((), (), s32[]{:S(2)}) async-start(), calls=%async_computation.5 | async-start | bytes 5013504 | tf_op jit(solution)/shard_map/all_gather | solution.py:86
  297.4 95.9 %reduce-scatter.12.cloned.1.call-start = ((), (), s32[]{:S(2)}) async-start(), calls=%async_computation.8 | async-start | bytes 1179648
Sparse Core Ops, SparseCore 0:
  47.3 57.6 all-gather.6
  111.4 30.7 reduce-scatter.9
  178.9 116.2 reduce-scatter.7
  297.9 57.7 all-gather.4
  362.5 30.7 reduce-scatter.11

commit v2 on v1

--- a/solution.py
+++ b/solution.py
@@ -1,39 +1,178 @@
+import functools
+
 import jax
 import jax.numpy as jnp
 from jax import lax
+from jax.experimental import pallas as pl
+from jax.experimental.pallas import tpu as pltpu
 from jax.sharding import PartitionSpec as P
 
+MESH = pl.DeviceIdType.MESH
+KV = 512
+GROUPS = 8
+score_scale = 192.0 ** (-0.5)
+
+
+def attend_kernel(
+    length_ref, partner_ref, slot_ref, query_ref, cache_ref, up_ref, out_ref,
+    query_buf, cache_buf, up_buf, lat_out, lat_in, wide, vals,
+    load_sem, up_sem, own_sem, send_sem, recv_sem,
+):
+    g = lax.axis_index("dp")
+    t = lax.axis_index("tp")
+    slots = query_ref.shape[0]
+    heads = up_ref.shape[0]
+
+    def loads(r):
+        return (
+            pltpu.make_async_copy(query_ref.at[r], query_buf.at[r], load_sem.at[0, r]),
+            pltpu.make_async_copy(cache_ref.at[r], cache_buf.at[r], load_sem.at[1, r]),
+        )
+
+    for r in range(slots):
+        for copy in loads(r):
+            copy.start()
+    up_copy = pltpu.make_async_copy(up_ref, up_buf, up_sem)
+    up_copy.start()
+    barrier = pltpu.get_barrier_semaphore()
+    for k in range(1, GROUPS):
+        pl.semaphore_signal(
+            barrier, inc=1, device_id=(lax.rem(g + k, GROUPS), t), device_id_type=MESH
+        )
+    pl.semaphore_wait(barrier, GROUPS - 1)
+
+    def send(k, r):
+        p = lax.rem(g + k, GROUPS)
+        return pltpu.make_async_remote_copy(
+            src_ref=lat_out.at[pl.ds(r, 2), pl.ds(pl.multiple_of(p * heads, heads), heads)],
+            dst_ref=lat_in.at[g, pl.ds(r, 2)],
+            send_sem=send_sem.at[k],
+            recv_sem=recv_sem.at[g],
+            device_id=(p, t),
+            device_id_type=MESH,
+        )
+
+    def attend(r):
+        for copy in loads(r):
+            copy.wait()
+        length = length_ref[g, r]
+        cache = cache_buf[r]
+        scores = lax.dot_general(
+            query_buf[r], cache, (((0,), (0,)), ((), ())), preferred_element_type=jnp.float32
+        )
+        position = lax.broadcasted_iota(jnp.int32, scores.shape, 1)
+        masked = jnp.where(position < length, scores * score_scale, -jnp.inf)
+        largest = jnp.max(masked, axis=1, keepdims=True)
+        expterm = jnp.exp(masked - largest)
+        total = jnp.sum(expterm, axis=1, keepdims=True)
+        weights = (expterm / total).astype(jnp.bfloat16)
+        latent = lax.dot_general(
+            weights, cache[:KV], (((1,), (1,)), ((), ())), preferred_element_type=jnp.float32
+        )
+        lat_out[r] = latent.astype(jnp.bfloat16)
+
+    def pair(i, carry):
+        attend(2 * i)
+        attend(2 * i + 1)
+        for k in (4, 3, 5, 2, 6, 1, 7):
+            send(k, 2 * i).start()
+        return carry
+
+    lax.fori_loop(0, slots // 2, pair, 0)
+    own = pltpu.make_async_copy(
+        lat_out.at[:, pl.ds(pl.multiple_of(g * heads, heads), heads)], lat_in.at[g], own_sem
+    )
+    own.start()
+    own.wait()
+    up_copy.wait()
+
+    def widen(k, carry):
+        s = lax.rem(g + k, GROUPS)
+
+        @pl.when(k > 0)
+        def _():
+            pltpu.make_async_remote_copy(
+                src_ref=lat_in.at[s], dst_ref=lat_in.at[s], send_sem=send_sem.at[0],
+                recv_sem=recv_sem.at[s], device_id=(s, t), device_id_type=MESH,
+            ).wait_recv()
+
+        rows = slots * heads
+        block = lat_in[s].astype(jnp.float32).reshape(rows, KV)
+        for lane in range(KV // 128):
+            wide[lane, pl.ds(pl.multiple_of(s * rows, rows), rows)] = block[
+                :, lane * 128 : (lane + 1) * 128
+            ]
+        return carry
+
+    lax.fori_loop(0, GROUPS, widen, 0)
+    count = GROUPS * slots
+    for h in range(heads):
+        head_rows = jnp.concatenate(
+            [wide[lane, pl.ds(h, count, stride=heads), :] for lane in range(KV // 128)], axis=1
+        )
+        vals[:, h * 128 : (h + 1) * 128] = jnp.dot(
+            head_rows.astype(jnp.bfloat16),
+            up_buf[h],
+            preferred_element_type=jnp.float32,
+        ).astype(jnp.bfloat16)
+    row = lax.broadcasted_iota(jnp.int32, (count, count), 0)
+    column = lax.broadcasted_iota(jnp.int32, (count, count), 1)
+    source = row
+    for group in range(GROUPS):
+        partner = partner_ref[group]
+        own_row = group * slots + slot_ref[group]
+        source = jnp.where(row == own_row, partner * slots + slot_ref[partner], source)
+    place = jnp.where(column == source, 1.0, 0.0).astype(jnp.bfloat16)
+    out_ref[...] = jnp.dot(place, vals[...], preferred_element_type=jnp.float32).astype(
+        jnp.bfloat16
+    )
+    for k in range(1, GROUPS):
+        pltpu.make_async_remote_copy(
+            src_ref=lat_in.at[0], dst_ref=lat_in.at[0], send_sem=send_sem.at[k],
+            recv_sem=recv_sem.at[0], device_id=(lax.rem(g + k, GROUPS), t), device_id_type=MESH,
+        ).wait_send()
+
+
+def attend_values(lengths, dest_group, moved_slot, queries, kv_cache, up_value):
+    slots, all_heads, _ = queries.shape
+    queries = jnp.swapaxes(queries, 1, 2)
+    kv_cache = jnp.swapaxes(kv_cache, 1, 2)
+    heads = up_value.shape[0]
+    rows = GROUPS * slots
+    smem = pl.BlockSpec(memory_space=pltpu.SMEM)
+    hbm = pl.BlockSpec(memory_space=pl.ANY)
+    bf16 = jnp.bfloat16
+    return pl.pallas_call(
+        attend_kernel,
+        name="attend",
+        out_shape=jax.ShapeDtypeStruct((rows, heads * 128), bf16),
+        in_specs=[smem, smem, smem, hbm, hbm, hbm],
+        out_specs=pl.BlockSpec(memory_space=pltpu.VMEM),
+        scratch_shapes=[
+            pltpu.VMEM(queries.shape, bf16),
+            pltpu.VMEM(kv_cache.shape, bf16),
+            pltpu.VMEM(up_value.shape, bf16),
+            pltpu.VMEM((slots, all_heads, KV), bf16),
+            pltpu.VMEM((GROUPS, slots, heads, KV), bf16),
+            pltpu.VMEM((KV // 128, GROUPS * slots * heads, 128), jnp.float32),
+            pltpu.VMEM((rows, heads * 128), bf16),
+            pltpu.SemaphoreType.DMA((2, slots)),
+            pltpu.SemaphoreType.DMA,
+            pltpu.SemaphoreType.DMA,
+            pltpu.SemaphoreType.DMA((GROUPS,)),
+            pltpu.SemaphoreType.DMA((GROUPS,)),
+        ],
+        compiler_params=pltpu.CompilerParams(
+            collective_id=0, has_side_effects=True, vmem_limit_bytes=56 << 20
+        ),
+        cost_estimate=pl.CostEstimate(
+            flops=2 * slots * all_heads * 1024 * 1088, bytes_accessed=13 << 20, transcendentals=1 << 20
+        ),
+    )(lengths[:, 0, :], dest_group[:, 0], moved_slot[:, 0], queries, kv_cache, up_value)
+
+
 D = 7168
-KV = 512
-
-
-score_scale = 192.0 ** (-0.5)
 norm_eps = 1e-06
-
-
-def attend_block(query_rows, cache_rows, length_rows):
-    scores = (
-        jnp.einsum("rhc,rkc->rhk", query_rows, cache_rows, preferred_element_type=jnp.float32)
-        * score_scale
-    )
-    position = lax.broadcasted_iota(jnp.int32, scores.shape, 2)
-    allowed = position < length_rows[:, None, None]
-    masked = jnp.where(allowed, scores, -jnp.inf)
-    largest = jnp.max(masked, axis=2, keepdims=True)
-    expterm = jnp.where(allowed, jnp.exp(masked - largest), 0.0)
-    weights = (expterm / jnp.sum(expterm, axis=2, keepdims=True)).astype(jnp.bfloat16)
-    latent = jnp.einsum(
-        "rhk,rkc->rhc", weights, cache_rows[:, :, :KV], preferred_element_type=jnp.float32
-    )
-    return latent.astype(jnp.bfloat16)
-
-
-def placed_sources(partners, slots, slot_count):
-    groups = jnp.arange(partners.shape[0], dtype=jnp.int32)[:, None]
-    slot_ids = jnp.arange(slot_count, dtype=jnp.int32)[None, :]
-    incoming = partners[:, None] * slot_count + slots[partners][:, None]
-    staying = groups * slot_count + slot_ids
-    return jnp.where(slot_ids == slots[:, None], incoming, staying).reshape(-1)
 
 
 def shards(
@@ -50,15 +189,7 @@
     up_proj,
     down_proj,
 ):
-    group = lax.axis_index("dp")
-    own_lengths = lax.dynamic_index_in_dim(lengths[:, 0, :], group, 0, keepdims=False)
-    latent = attend_block(queries, kv_cache, own_lengths)
-    head_rows = lax.all_to_all(latent, "dp", split_axis=1, concat_axis=0, tiled=True)
-    values = jnp.einsum(
-        "rhc,hcd->rhd", head_rows, up_value, preferred_element_type=jnp.float32
-    ).astype(jnp.bfloat16)
-    values = values.reshape(values.shape[0], values.shape[1] * values.shape[2])
-    values = values[placed_sources(dest_group[:, 0], moved_slot[:, 0], own_lengths.shape[0])]
+    values = attend_values(lengths, dest_group, moved_slot, queries, kv_cache, up_value)
     head_terms = jnp.dot(
         lax.all_gather(values, "tp", axis=0, tiled=True),
         out_proj,

time: 408 us -> 388 us (0.951)
  Pallas kernels: 0 us -> 21 us
  matrix products: 34.6 us -> 16 us
  waiting for transfers between devices: 247 us -> 236 us
  starting transfers between devices: 5.45 us -> 0.21 us
  local copies, waits for them, and re-layouts: 10.5 us -> 5.88 us
    pallas_call x0 -> x1, Pallas kernels: none -> 21 us  [attend_values(): pl.pallas_call(attend_kernel, name='attend', out_shape=jax.ShapeDtypeStru...]
    all_to_all x1 -> x0, waiting for transfers between devices: 13.1 us -> none  [shards(): lax.all_to_all(latent, 'dp', split_axis=1, concat_axis=0, tiled=True)]
    sub x1 -> x0, matrix products: 8.83 us -> none  [attend_block(): expterm = jnp.where(allowed, jnp.exp(masked - largest), 0.0)]
    dot_general x2 -> x0, matrix products: 8.03 us -> none  [the longest x1 7.56 us: attend_block(): jnp.einsum('rhk,rkc->rhc', weights, cache_rows[:, :, :KV], preferred_elem...]
    all_to_all x1 -> x0, starting transfers between devices: 5.28 us -> none  [shards(): lax.all_to_all(latent, 'dp', split_axis=1, concat_axis=0, tiled=True)]
  transfers between devices with their start and end apart: 6 -> 5, of which waited for: 6 -> 5; matrix products, arithmetic and copies ran while one was open for 0% -> 0% of each run, Pallas kernels for 0% -> 0%
where the time goes in v2:
time: 388 us; the launch traced here: 382 us
  waiting for transfers between devices  236 us (61%)
  blocking collectives  80.8 us (21%)
  Pallas kernels  21 us (5%)
  matrix products  16 us (4%)
  between operations  14.5 us (4%)
  other arithmetic  7.73 us (2%)
  local copies, waits for them, and re-layouts  5.88 us (2%)
    unnamed x7, waiting for transfers between devices  62.7 us
    all_gather x1, waiting for transfers between devices, shards(): lax.all_gather(values, 'tp', axis=0, tiled=True)  58.4 us
    all_gather x1, waiting for transfers between devices, shards(): hidden = lax.all_gather(hidden, 'tp', axis=0, tiled=True)  58.2 us
    reduce_scatter x1, waiting for transfers between devices, shards(): lax.psum_scatter(partial_gate.astype(jnp.bfloat16), 'tp', scatter_dimensi...  56.4 us
    unnamed x1, blocking collectives  46.4 us
    all_gather x1, blocking collectives, shards(): block_rows = lax.all_gather(scaled, 'dp', axis=0, tiled=True)  23.1 us
    pallas_call x1, Pallas kernels, attend_values(): pl.pallas_call(attend_kernel, name='attend', out_shape=jax.ShapeDtypeStru...  21 us
    all_gather x1, blocking collectives, shards(): block_sums = lax.all_gather(square_sum, 'dp', axis=0, tiled=True)  11.3 us
  transfers between devices with their start and end apart: 5, of which 5 were waited for; matrix products, arithmetic and copies ran while one was open for 0% of the time, Pallas kernels for 0%

profile of v2, /device:TPU:3, one launch (start us, length us, event | category | flops | bytes accessed | tf_op | source)
XLA Modules:
  0.0 381.8 jit_solution(2184645217539237155)
XLA Ops:
  7.2 21.0 %attend.1 = bf16[64,2048]{1,0:T(8,128)(2,1)} custom-call(s32[8,8]{1,0:T(8,128)} %bitcast.21, s32[8]{0:T(128)} %bitcast.23, s32[8]{0:T(128)} %bitcast.24, bf16[8,576,128]{2,1,0:T(8,128)(2,1)} %bitcast.19, bf16[8,576,1024]{2,1,0:T(8,128)(2,1)} %bitcast.18, bf16[16,512,128]{2,1,0:T(8,128)(2,1)} %up_ref.1), custom_call_target="tpu_custom_call" | custom-call | flops 2281701376 | bytes 13631488 | tf_op jit(solution)/shard_map/attend/pallas_call | solution.py:145
  28.3 58.4 %all-gather.4.cloned.1.call-done = bf16[1024,2048]{1,0:T(8,128)(2,1)} async-done(((bf16[64,2048]{1,0:T(8,128)(2,1)}), bf16[1024,2048]{1,0:T(8,128)(2,1)}) %all-gather.4.cloned.1.call-update) | async-done | bytes 4194320 | tf_op jit(solution)/shard_map/all_gather | solution.py:194
  86.7 4.9 %convolution_convert_fusion.3 = bf16[1024,448]{0,1:T(8,128)(2,1)S(1)} fusion(bf16[1024,2048]{1,0:T(8,128)(2,1)} %all-gather.4.cloned.1.call-done, bf16[2048,448]{0,1:T(8,128)(2,1)} %param.20), kind=kOutput, calls=%fused_computation.4 | convolution fusion | flops 1879506944 | bytes 6946816 | tf_op jit(solution)/shard_map/dot_general | solution.py:193
  91.6 1.3 copy.14
  93.0 31.2 %reduce-scatter.10.cloned.1.call-done = bf16[128,448]{1,0:T(8,128)(2,1)} async-done(((bf16[1024,448]{1,0:T(8,128)(2,1)}), bf16[128,448]{1,0:T(8,128)(2,1)}) %reduce-scatter.10.cloned.1.call-update) | async-done | bytes 114704
  124.2 1.0 copy.15
  125.3 0.1 multiply_reduce_fusion
  125.4 23.1 %all_gather.13 = bf16[1024,448]{0,1:T(8,128)(2,1)S(1)} all-gather(bf16[128,448]{0,1:T(8,128)(2,1)S(1)} %get-tuple-element.3), channel_id=1, replica_groups=mesh['dp'=8,'tp'=16] {'dp'}, dimensions={0}, use_global_device_ids=true | all-gather | bytes 1032192 | tf_op jit(solution)/shard_map/all_gather | solution.py:204
  148.5 2.9 convolution_convert_fusion
  151.4 2.9 convolution_convert_fusion.1
  154.3 4.7 %pad_maximum_fusion = bf16[1024,4608]{1,0:T(8,128)(2,1)} fusion(bf16[1024,2304]{1,0:T(8,128)(2,1)S(1)} %convolution_convert_fusion, bf16[1024,2304]{1,0:T(8,128)(2,1)S(1)} %convolution_convert_fusion.1), kind=kLoop, calls=%fused_computation | loop fusion | flops 18874368 | bytes 18874368 | tf_op jit(solution)/shard_map/concatenate | solution.py:208
  159.1 0.6 copy-done.5
  159.7 0.6 dynamic-slice
  160.9 11.3 %all-gather = f32[8,1,128]{2,1,0:T(1,128)S(1)} all-gather(f32[1,1,128]{2,1,0:T(1,128)S(1)} %bitcast.22), channel_id=1, replica_groups=mesh['dp'=8,'tp'=16] {'dp'}, dimensions={0}, use_global_device_ids=true | all-gather | bytes 4608 | tf_op jit(solution)/shard_map/all_gather | solution.py:205
  172.2 46.4 %all-reduce = f32[1024]{0:T(1024)S(1)} all-reduce(f32[1024]{0:T(1024)S(1)} %bitcast.20), channel_id=4, replica_groups=mesh['dp'=8,'tp'=16] {'tp'}, use_global_device_ids=true, to_apply=%region_3.0.clone | all-reduce | flops 1024 | bytes 8192
  218.7 56.4 %reduce-scatter.8.cloned.1.call-done = bf16[64,4608]{1,0:T(8,128)(2,1)} async-done(((bf16[1024,4608]{1,0:T(8,128)(2,1)}), bf16[64,4608]{1,0:T(8,128)(2,1)}) %reduce-scatter.8.cloned.1.call-update) | async-done | bytes 589840 | tf_op jit(solution)/shard_map/reduce_scatter | solution.py:210
  275.1 1.2 convert_multiply_fusion
  276.3 0.9 fusion
  277.3 58.2 %all-gather.6.cloned.1.call-done = bf16[1024,2304]{1,0:T(8,128)(2,1)} async-done(((bf16[64,2304]{1,0:T(8,128)(2,1)}), bf16[1024,2304]{1,0:T(8,128)(2,1)}) %all-gather.6.cloned.1.call-update) | async-done | bytes 4718608 | tf_op jit(solution)/shard_map/all_gather | solution.py:217
  335.4 5.3 %convolution_convert_fusion.2 = bf16[1024,448]{0,1:T(8,128)(2,1)S(1)} fusion(bf16[1024,2304]{1,0:T(8,128)(2,1)} %all-gather.6.cloned.1.call-done, bf16[2304,448]{0,1:T(8,128)(2,1)} %param.23), kind=kOutput, calls=%fused_computation.3 | convolution fusion | flops 2114387968 | bytes 7700480 | tf_op jit(solution)/shard_map/dot_general | solution.py:220
  340.8 1.3 copy.16
  342.1 31.4 %reduce-scatter.12.cloned.1.call-done = bf16[128,448]{1,0:T(8,128)(2,1)} async-done(((bf16[1024,448]{1,0:T(8,128)(2,1)}), bf16[128,448]{1,0:T(8,128)(2,1)}) %reduce-scatter.12.cloned.1.call-update) | async-done | bytes 114704
  373.5 1.0 copy.17
  374.6 0.7 add_convert_fusion
  (23 shorter events, 0.4 us)
Async XLA Ops:
  7.2 141.3 %copy-start = (bf16[448,2304]{1,0:T(8,128)(2,1)S(1)}, bf16[448,2304]{1,0:T(8,128)(2,1)}, u32[]{:S(2)}) copy-start(bf16[448,2304]{1,0:T(8,128)(2,1)} %param.22) | copy-start | bytes 6193156
  7.2 79.5 %all-gather.4.cloned.1.call-start = ((), (), s32[]{:S(2)}) async-start(), calls=%async_computation.3 | async-start | bytes 4456448 | tf_op jit(solution)/shard_map/all_gather | solution.py:194
  28.3 95.9 %reduce-scatter.10.cloned.1.call-start = ((), (), s32[]{:S(2)}) async-start(), calls=%async_computation.6 | async-start | bytes 1179648
  91.6 1.4 copy-start.3
  91.6 33.7 %copy-start.2 = (bf16[128,448]{0,1:T(8,128)(2,1)S(1)}, bf16[128,448]{0,1:T(8,128)(2,1)}, u32[]{:S(2)}) copy-start(bf16[128,448]{0,1:T(8,128)(2,1)} %param.17) | copy-start | bytes 344068
  92.9 182.2 %reduce-scatter.8.cloned.1.call-start = ((), (), s32[]{:S(2)}) async-start(), calls=%async_computation.4 | async-start | bytes 10027008 | tf_op jit(solution)/shard_map/reduce_scatter | solution.py:210
  125.3 249.3 %copy-start.1 = (bf16[128,448]{0,1:T(8,128)(2,1)}, bf16[128,448]{0,1:T(8,128)(2,1)S(1)}, u32[]{:S(2)}) copy-start(bf16[128,448]{0,1:T(8,128)(2,1)S(1)} %copy.15) | copy-start | bytes 344068
  148.5 2.9 copy-start.4
  159.0 0.7 copy-start.5
  159.0 176.4 %all-gather.6.cloned.1.call-start = ((), (), s32[]{:S(2)}) async-start(), calls=%async_computation.5 | async-start | bytes 5013504 | tf_op jit(solution)/shard_map/all_gather | solution.py:217
  277.2 96.3 %reduce-scatter.12.cloned.1.call-start = ((), (), s32[]{:S(2)}) async-start(), calls=%async_computation.7 | async-start | bytes 1179648
Sparse Core Ops, SparseCore 0:
  28.4 58.2 all-gather.3
  93.1 31.1 reduce-scatter.9
  159.1 115.9 reduce-scatter.7
  277.7 57.6 all-gather.5
  342.2 31.2 reduce-scatter.11

commit v3 on v2

--- a/solution.py
+++ b/solution.py
@@ -1,5 +1,3 @@
-import functools
-
 import jax
 import jax.numpy as jnp
 from jax import lax
@@ -173,6 +171,385 @@
 
 D = 7168
 norm_eps = 1e-06
+A_EXTRA = 512
+
+
+def layer_kernel(
+    vals_ref, resid_ref, gain_ref, wo_ref, wg_ref, wu_ref, wd_ref, attended_ref, out_ref,
+    wo, wg, wu, wd, resid_both, gain_own, gain_both,
+    vb, c_out, c_in, xb, part_a, part_b, a1_in, a2_out, a2_in, b1_in, b2_out, b2_in, b_keep,
+    hb, g_out, g_in, resid_rows, att_x, lay_x, turned,
+    w_l, w_s, w_r, v_s, v_r, c_s, c_r, x_s, x_r, a1_s, a1_r, a2_s, a2_r, b1_s, b1_r, b2_s, b2_r,
+    h_s, h_r, g_s, g_r, o_s, o_r,
+):
+    g = lax.axis_index("dp")
+    t = lax.axis_index("tp")
+    c = lax.rem(t, 2)
+    q = t // 2
+    z = q // 2
+    yh = lax.rem(q, 2)
+    x = g // 2
+    rows = vals_ref.shape[0]
+    feats = wo_ref.shape[0]
+    ff = wg_ref.shape[1]
+    both = 2 * feats
+    a_cols = ff + A_EXTRA
+    b_cols = ff - A_EXTRA
+    half = rows // 2
+    f32 = jnp.float32
+    bf16 = jnp.bfloat16
+
+    def other_group(k):
+        return (lax.rem(g + k, GROUPS), t)
+
+    def other_z(k):
+        return (g, lax.rem(z + k, 4) * 4 + yh * 2 + c)
+
+    def chip(zp):
+        return (g, zp * 4 + yh * 2 + c)
+
+    y_peer = (g, z * 4 + (1 - yh) * 2 + c)
+    sibling = (g, q * 2 + 1 - c)
+
+    def remote(src, dst, send_sem, recv_sem, device):
+        return pltpu.make_async_remote_copy(
+            src_ref=src, dst_ref=dst, send_sem=send_sem, recv_sem=recv_sem,
+            device_id=device, device_id_type=MESH,
+        )
+
+    def arrived(ref, sem):
+        remote(ref, ref, sem, sem, sibling).wait_recv()
+
+    def left(ref, sem):
+        remote(ref, ref, sem, sem, sibling).wait_send()
+
+    def order(i):
+        return i + (i // 2) * (5 - 2 * i)
+
+    barrier = pltpu.get_barrier_semaphore()
+    greeted = [other_group(k) for k in range(1, GROUPS)]
+    greeted += [other_z(k) for k in (1, 2, 3)] + [y_peer, sibling]
+    for device in greeted:
+        pl.semaphore_signal(barrier, inc=1, device_id=device, device_id_type=MESH)
+
+    own_rows = pl.ds(pl.multiple_of(c * feats, feats), feats)
+    gain_own[...] = jnp.transpose(
+        jnp.broadcast_to(gain_ref[...].astype(f32), (128, feats)), (1, 0)
+    ).astype(bf16)
+    weights = (
+        (wo_ref, wo), (resid_ref, resid_both), (gain_own, gain_both),
+        (wg_ref, wg), (wu_ref, wu), (wd_ref, wd),
+    )
+    for i, (src, dst) in enumerate(weights):
+        pltpu.make_async_copy(src, dst.at[own_rows], w_l.at[i]).start()
+    vb[q] = vals_ref[...]
+    pl.semaphore_wait(barrier, len(greeted))
+
+    upper = pl.ds(0, half)
+    lower = pl.ds(half, half)
+
+    def gather_start(buf, s, r):
+        own_a = buf.at[q, upper]
+        own_b = buf.at[q, lower]
+        remote(own_a, own_a, s.at[0], r.at[0], y_peer).start()
+        for k in (2, 1, 3):
+            remote(own_b, own_b, s.at[k], r.at[k], other_z(k)).start()
+        remote(own_b, own_b, s.at[10], r.at[10], y_peer).start()
+        for k in (2, 1, 3):
+            remote(own_a, own_a, s.at[3 + k], r.at[3 + k], other_z(k)).start()
+
+    def forward_y(buf, s, r):
+        block = buf.at[z * 2 + 1 - yh, upper]
+        arrived(block, r.at[0])
+        for k in (2, 1, 3):
+            remote(block, block, s.at[6 + k], r.at[6 + k], other_z(k)).start()
+
+    def forward_z(buf, s, r, k):
+        block = buf.at[lax.rem(z + 4 - k, 4) * 2 + yh, lower]
+        arrived(block, r.at[k])
+        remote(block, block, s.at[10 + k], r.at[10 + k], y_peer).start()
+
+    def project(buf, w, s, r, out, landed, out_s, out_r):
+        forward_y(buf, s, r)
+        forward_z(buf, s, r, 1)
+        forward_z(buf, s, r, 3)
+
+        def step(i, carry):
+            k = order(i)
+            zp = lax.rem(z + 4 - k, 4)
+            arrived(buf.at[0, lower], r.at[10 + k])
+
+            @pl.when(k > 0)
+            def _():
+                arrived(buf.at[0, upper], r.at[3 + k])
+                arrived(buf.at[0, upper], r.at[6 + k])
+
+            left_rows = buf[pl.ds(2 * zp, 2)].reshape(2 * rows, buf.shape[2])
+            product = lax.dot_general(
+                left_rows, w[...], (((1,), (1,)), ((), ())), preferred_element_type=f32
+            )
+            out[pl.ds(2 * zp, 2)] = product.astype(bf16).reshape(2, rows, both)
+            for j in range(2):
+                d = 2 * zp + j
+
+                @pl.when(d != g)
+                def _():
+                    remote(out.at[d], landed.at[g], out_s.at[d], out_r.at[g], (d, t)).start()
+
+            @pl.when(i == 0)
+            def _():
+                forward_z(buf, s, r, 2)
+
+            return carry
+
+        lax.fori_loop(0, 4, step, 0)
+
+    def gathered_sum(out, landed, out_r):
+        total = out[g].astype(f32)
+        for k in range(1, GROUPS):
+            d = lax.rem(g + k, GROUPS)
+            arrived(landed.at[d], out_r.at[d])
+            total += landed[d].astype(f32)
+        return total
+
+    def finish_gather(buf, s):
+        for i in range(14):
+            left(buf.at[0, upper], s.at[i])
+
+    def finish_sends(out, out_s):
+        for k in range(1, GROUPS):
+            left(out.at[0], out_s.at[lax.rem(g + k, GROUPS)])
+
+    def with_sum(square_sum):
+        high = square_sum.astype(bf16).astype(f32)
+        lane = lax.broadcasted_iota(jnp.int32, (square_sum.shape[0], 128), 1)
+        return jnp.where(
+            lane == 0, high, jnp.where(lane == 1, square_sum - high, 0.0)
+        ).astype(bf16)
+
+    def placed(exchange, target):
+        stacked = exchange[...].reshape(2 * rows, both).astype(f32)
+        turned[...] = jnp.transpose(stacked, (1, 0))
+        target[...] = turned[own_rows].astype(bf16)
+
+    gather_start(vb, v_s, v_r)
+    for i, (src, dst) in enumerate(weights):
+        remote(src, dst.at[own_rows], w_s.at[i], w_r.at[i], sibling).start()
+
+    def weight_ready(i):
+        src, dst = weights[i]
+        pltpu.make_async_copy(src, dst.at[own_rows], w_l.at[i]).wait()
+        arrived(dst.at[own_rows], w_r.at[i])
+
+    for i in range(3):
+        weight_ready(i)
+    mine = pl.ds(pl.multiple_of(c * rows, rows), rows)
+    turned[...] = resid_both[...].astype(f32)
+    resid_rows[...] = jnp.transpose(turned[...], (1, 0))
+    project(vb, wo, v_s, v_r, c_out, c_in, c_s, c_r)
+    attn = gathered_sum(c_out, c_in, c_r)
+    att_x[c] = attn.astype(bf16)
+    remote(att_x.at[c], att_x.at[c], o_s.at[0], o_r.at[0], sibling).start()
+    resid = resid_rows[mine] + attn
+    resid_rows[mine] = resid
+    gain = jnp.transpose(gain_both[...].astype(f32), (1, 0))[:1]
+    xb[g, :, :both] = (resid * gain).astype(bf16)
+    xb[g, :, both:] = with_sum(jnp.sum(resid * resid, axis=1, keepdims=True))
+    for k in (4, 3, 5, 2, 6, 1, 7):
+        remote(xb.at[g], xb.at[g], x_s.at[k], x_r.at[g], other_group(k)).start()
+    arrived(att_x.at[1 - c], o_r.at[0])
+    placed(att_x, attended_ref)
+    for i in range(3, 6):
+        weight_ready(i)
+
+    def first_products(i, carry):
+        xp = lax.rem(x + 4 - order(i), 4)
+        for j in range(2):
+            d = 2 * xp + j
+
+            @pl.when(d != g)
+            def _():
+                arrived(xb.at[d], x_r.at[d])
+
+        block = xb[pl.ds(2 * xp, 2)].reshape(2 * rows, both + 128)
+        pair = pl.ds(2 * xp, 2)
+        lhs = block[:, :both]
+
+        def product(w, start, width):
+            return jnp.dot(
+                lhs, w[:, start : start + width], preferred_element_type=f32
+            ).astype(bf16).reshape(2, rows, width)
+
+        for n in range(0, ff, 768):
+            part_a[pair, :, n : n + 768] = product(wg, n, 768)
+        part_a[pair, :, ff:] = product(wu, 0, A_EXTRA)
+        remote(
+            part_a.at[2 * xp + 1 - yh], a1_in.at[xp], a1_s.at[xp], a1_r.at[xp], y_peer
+        ).start()
+        for n in range(0, b_cols, 896):
+            part_b[pair, :, n : n + 896] = product(wu, A_EXTRA + n, 896)
+        part_b[pair, :, b_cols:] = block[:, both:].reshape(2, rows, 128)
+
+        @pl.when(xp != z)
+        def _():
+            remote(part_b.at[pair], b1_in.at[z], b1_s.at[xp], b1_r.at[z], chip(xp)).start()
+
+        return carry
+
+    lax.fori_loop(0, 4, first_products, 0)
+
+    def second_a(i, carry):
+        xp = lax.rem(x + 4 - order(i), 4)
+        arrived(a1_in.at[xp], a1_r.at[xp])
+        a2_out[xp] = (
+            part_a[2 * xp + yh].astype(f32) + a1_in[xp].astype(f32)
+        ).astype(bf16)
+
+        @pl.when(xp != z)
+        def _():
+            remote(a2_out.at[xp], a2_in.at[z], a2_s.at[xp], a2_r.at[z], chip(xp)).start()
+
+        return carry
+
+    lax.fori_loop(0, 3, second_a, 0)
+    for k in (1, 3, 2):
+        s = lax.rem(z + k, 4)
+        arrived(b1_in.at[s], b1_r.at[s])
+
+    def sum_b(j):
+        total = part_b[2 * z + j].astype(f32)
+        for k in (1, 2, 3):
+            total += b1_in[lax.rem(z + k, 4), j].astype(f32)
+        return total
+
+    def total_squares(block):
+        return block[:, b_cols : b_cols + 1] + block[:, b_cols + 1 : b_cols + 2]
+
+    away = sum_b(1 - yh)
+    b2_out[:, :b_cols] = away[:, :b_cols].astype(bf16)
+    b2_out[:, b_cols:] = with_sum(total_squares(away))
+    remote(b2_out, b2_in, b2_s.at[0], b2_r.at[0], y_peer).start()
+    b_keep[...] = sum_b(yh)
+    lax.fori_loop(3, 4, second_a, 0)
+    arrived(b2_in, b2_r.at[0])
+    for k in (1, 3, 2):
+        s = lax.rem(z + k, 4)
+        arrived(a2_in.at[s], a2_r.at[s])
+
+    def sum_a(start, width):
+        cols = slice(start, start + width)
+        total = a2_out[z, :, cols].astype(f32)
+        for k in (1, 2, 3):
+            total += a2_in[lax.rem(z + k, 4), :, cols].astype(f32)
+        return total
+
+    def sum_b2(start, width):
+        cols = slice(start, start + width)
+        return b_keep[:, cols] + b2_in[:, cols].astype(f32)
+
+    square_sum = total_squares(jnp.concatenate(
+        [jnp.zeros((rows, b_cols), f32), sum_b2(b_cols, 128)], axis=1
+    ))
+    scale = lax.rsqrt(square_sum / D + norm_eps)
+
+    def write_hidden(start, width, upward):
+        gate = sum_a(start, width) * scale
+        hb[q, :, start : start + width] = (
+            gate / (1.0 + jnp.exp(-gate)) * (upward * scale)
+        ).astype(bf16)
+
+    write_hidden(0, A_EXTRA, sum_a(ff, A_EXTRA))
+    for n in range(0, b_cols, 896):
+        write_hidden(A_EXTRA + n, 896, sum_b2(n, 896))
+    gather_start(hb, h_s, h_r)
+    project(hb, wd, h_s, h_r, g_out, g_in, g_s, g_r)
+    down = gathered_sum(g_out, g_in, g_r)
+    lay_x[c] = (resid_rows[mine] + down).astype(bf16)
+    remote(lay_x.at[c], lay_x.at[c], o_s.at[1], o_r.at[1], sibling).start()
+    arrived(lay_x.at[1 - c], o_r.at[1])
+    placed(lay_x, out_ref)
+
+    for i, (src, dst) in enumerate(weights):
+        left(src, w_s.at[i])
+    finish_gather(vb, v_s)
+    finish_gather(hb, h_s)
+    finish_sends(c_out, c_s)
+    finish_sends(g_out, g_s)
+    for k in range(1, GROUPS):
+        left(xb.at[0], x_s.at[k])
+    for i in range(4):
+        left(part_a.at[0], a1_s.at[i])
+    for k in (1, 2, 3):
+        s = lax.rem(z + k, 4)
+        left(b1_in.at[0], b1_s.at[s])
+        left(a2_out.at[0], a2_s.at[s])
+    left(b2_out, b2_s.at[0])
+    left(att_x.at[0], o_s.at[0])
+    left(lay_x.at[0], o_s.at[1])
+
+
+def run_layer(values, residual_in, norm_gain, out_proj, gate_proj, up_proj, down_proj):
+    rows, width = values.shape
+    total_rows, feats = residual_in.shape
+    ff = gate_proj.shape[1]
+    both = 2 * feats
+    a_cols, b_cols = ff + A_EXTRA, ff - A_EXTRA + 128
+    f32, bf16 = jnp.float32, jnp.bfloat16
+    vmem = pl.BlockSpec(memory_space=pltpu.VMEM)
+    hbm = pl.BlockSpec(memory_space=pl.ANY)
+    dma = pltpu.SemaphoreType.DMA
+    block = jax.ShapeDtypeStruct((feats, total_rows), bf16)
+    attended, layer_out = pl.pallas_call(
+        layer_kernel,
+        name="layer",
+        out_shape=(block, block),
+        in_specs=[vmem, vmem, vmem, hbm, hbm, hbm, hbm],
+        out_specs=(vmem, vmem),
+        scratch_shapes=[
+            pltpu.VMEM((both, width), bf16),
+            pltpu.VMEM((both, ff), bf16),
+            pltpu.VMEM((both, ff), bf16),
+            pltpu.VMEM((both, ff), bf16),
+            pltpu.VMEM((both, total_rows), bf16),
+            pltpu.VMEM((feats, 128), bf16),
+            pltpu.VMEM((both, 128), bf16),
+            pltpu.VMEM((8, rows, width), bf16),
+            pltpu.VMEM((8, rows, both), bf16),
+            pltpu.VMEM((8, rows, both), bf16),
+            pltpu.VMEM((8, rows, both + 128), bf16),
+            pltpu.VMEM((8, rows, a_cols), bf16),
+            pltpu.VMEM((8, rows, b_cols), bf16),
+            pltpu.VMEM((4, rows, a_cols), bf16),
+            pltpu.VMEM((4, rows, a_cols), bf16),
+            pltpu.VMEM((4, rows, a_cols), bf16),
+            pltpu.VMEM((4, 2, rows, b_cols), bf16),
+            pltpu.VMEM((rows, b_cols), bf16),
+            pltpu.VMEM((rows, b_cols), bf16),
+            pltpu.VMEM((rows, b_cols), f32),
+            pltpu.VMEM((8, rows, ff), bf16),
+            pltpu.VMEM((8, rows, both), bf16),
+            pltpu.VMEM((8, rows, both), bf16),
+            pltpu.VMEM((total_rows, both), f32),
+            pltpu.VMEM((2, rows, both), bf16),
+            pltpu.VMEM((2, rows, both), bf16),
+            pltpu.VMEM((both, total_rows), f32),
+            dma((6,)), dma((6,)), dma((6,)), dma((14,)), dma((14,)),
+            dma((8,)), dma((8,)), dma((8,)), dma((8,)),
+            dma((4,)), dma((4,)), dma((4,)), dma((4,)), dma((4,)), dma((4,)), dma((1,)), dma((1,)),
+            dma((14,)), dma((14,)), dma((8,)), dma((8,)), dma((2,)), dma((2,)),
+        ],
+        compiler_params=pltpu.CompilerParams(
+            collective_id=1, has_side_effects=True, vmem_limit_bytes=56 << 20
+        ),
+        cost_estimate=pl.CostEstimate(
+            flops=2 * total_rows * 8 * feats * (width + 3 * ff), bytes_accessed=10 << 20,
+            transcendentals=1 << 20,
+        ),
+    )(
+        values, jnp.swapaxes(residual_in, 0, 1), norm_gain[None, :], jnp.swapaxes(out_proj, 0, 1),
+        gate_proj, up_proj, jnp.swapaxes(down_proj, 0, 1),
+    )
+    return jnp.swapaxes(attended, 0, 1), jnp.swapaxes(layer_out, 0, 1)
 
 
 def shards(
@@ -190,39 +567,7 @@
     down_proj,
 ):
     values = attend_values(lengths, dest_group, moved_slot, queries, kv_cache, up_value)
-    head_terms = jnp.dot(
-        lax.all_gather(values, "tp", axis=0, tiled=True),
-        out_proj,
-        preferred_element_type=jnp.float32,
-    )
-    attn = lax.psum_scatter(
-        head_terms.astype(jnp.bfloat16), "dp", scatter_dimension=0, tiled=True
-    ).astype(jnp.float32)
-    resid = residual_in.astype(jnp.float32) + attn
-    square_sum = jnp.sum(resid * resid, axis=1)
-    scaled = (resid * norm_gain.astype(jnp.float32)).astype(jnp.bfloat16)
-    block_rows = lax.all_gather(scaled, "dp", axis=0, tiled=True)
-    block_sums = lax.all_gather(square_sum, "dp", axis=0, tiled=True)
-    gate_part = jnp.dot(block_rows, gate_proj, preferred_element_type=jnp.float32)
-    upward_part = jnp.dot(block_rows, up_proj, preferred_element_type=jnp.float32)
-    partial_gate = jnp.concatenate((gate_part, upward_part), axis=1)
-    ff_local = gate_proj.shape[1]
-    summed = lax.psum_scatter(
-        partial_gate.astype(jnp.bfloat16), "tp", scatter_dimension=0, tiled=True
-    ).astype(jnp.float32)
-    row_sums = lax.psum_scatter(block_sums, "tp", scatter_dimension=0, tiled=True)
-    row_scale = lax.rsqrt(row_sums / D + norm_eps)[:, None]
-    summed = summed * row_scale
-    hidden = (jax.nn.silu(summed[:, :ff_local]) * summed[:, ff_local:]).astype(jnp.bfloat16)
-    hidden = lax.all_gather(hidden, "tp", axis=0, tiled=True)
-    block_rows = hidden
-    down = lax.psum_scatter(
-        jnp.dot(block_rows, down_proj, preferred_element_type=jnp.float32).astype(jnp.bfloat16),
-        "dp",
-        scatter_dimension=0,
-        tiled=True,
-    ).astype(jnp.float32)
-    return (attn.astype(jnp.bfloat16), (resid + down).astype(jnp.bfloat16))
+    return run_layer(values, residual_in, norm_gain, out_proj, gate_proj, up_proj, down_proj)
 
 
 def solution(mesh):

time: 388 us -> 169 us (0.44)
  waiting for transfers between devices: 236 us -> 0 us
  Pallas kernels: 21 us -> 161 us
  blocking collectives: 80.8 us -> 0 us
  matrix products: 16 us -> 0 us
  between operations: 14.5 us -> 0.65 us
  other arithmetic: 7.73 us -> 0 us
    pallas_call x0 -> x1, Pallas kernels: none -> 140 us  [run_layer(): pl.pallas_call(layer_kernel, name='layer', out_shape=(block, block), in_s...]
    all_gather x2 -> x0, waiting for transfers between devices: 117 us -> none  [the longest x1 58.4 us: shards(): lax.all_gather(values, 'tp', axis=0, tiled=True)]
    unnamed x7 -> x0, waiting for transfers between devices: 62.7 us -> none
    reduce_scatter x1 -> x0, waiting for transfers between devices: 56.4 us -> none  [shards(): lax.psum_scatter(partial_gate.astype(jnp.bfloat16), 'tp', scatter_dimensi...]
    unnamed x1 -> x0, blocking collectives: 46.4 us -> none
    all_gather x2 -> x0, blocking collectives: 34.4 us -> none  [the longest x1 23.1 us: shards(): block_rows = lax.all_gather(scaled, 'dp', axis=0, tiled=True)]
    dot_general x4 -> x0, matrix products: 16 us -> none  [the longest x1 5.34 us: shards(): jnp.dot(block_rows, down_proj, preferred_element_type=jnp.float32)]
    concatenate x1 -> x0, other arithmetic: 4.71 us -> none  [shards(): partial_gate = jnp.concatenate((gate_part, upward_part), axis=1)]
  transfers between devices with their start and end apart: 5 -> 0, of which waited for: 5 -> 0; matrix products, arithmetic and copies ran while one was open for 0% -> 0% of each run, Pallas kernels for 0% -> 0%
where the time goes in v3:
time: 169 us; the launch traced here: 166 us
  Pallas kernels  161 us (95%)
  local copies, waits for them, and re-layouts  4.36 us (3%)
    pallas_call x1, Pallas kernels, run_layer(): pl.pallas_call(layer_kernel, name='layer', out_shape=(block, block), in_s...  140 us
    pallas_call x1, Pallas kernels, attend_values(): pl.pallas_call(attend_kernel, name='attend', out_shape=jax.ShapeDtypeStru...  20.8 us

profile of v3, /device:TPU:3, one launch (start us, length us, event | category | flops | bytes accessed | tf_op | source)
XLA Modules:
  0.0 166.1 jit_solution(287892333991949450)
XLA Ops:
  0.6 1.3 broadcast_in_dim.3.gain_ref
  1.9 20.8 %attend.1.vals_ref = bf16[64,2048]{1,0:T(8,128)(2,1)} custom-call(s32[8,8]{1,0:T(8,128)} %bitcast.14, s32[8]{0:T(128)} %bitcast.15, s32[8]{0:T(128)} %bitcast.16, bf16[8,576,128]{2,1,0:T(8,128)(2,1)} %bitcast.11, bf16[8,576,1024]{2,1,0:T(8,128)(2,1)} %bitcast.10, bf16[16,512,128]{2,1,0:T(8,128)(2,1)} %up_ref.1), custom_call_target="tpu_custom_call" | custom-call | flops 2281701376 | bytes 13631488 | tf_op jit(solution)/shard_map/attend/pallas_call | solution.py:143
  22.7 140.3 %layer.1 = (bf16[448,128]{1,0:T(8,128)(2,1)}, bf16[448,128]{1,0:T(8,128)(2,1)}) custom-call(bf16[64,2048]{1,0:T(8,128)(2,1)} %attend.1.vals_ref, bf16[448,128]{1,0:T(8,128)(2,1)} %bitcast.19, bf16[1,448]{1,0:T(2,128)(2,1)} %broadcast_in_dim.3.gain_ref, bf16[448,2048]{1,0:T(8,128)(2,1)} %bitcast.18, bf16[448,2304]{1,0:T(8,128)(2,1)} %wg_ref.1, ...), custom_call_target="tpu_custom_call" | custom-call | flops 8220835840 | bytes 10485760 | tf_op jit(solution)/shard_map/layer/pallas_call | solution.py:502
  163.0 1.6 copy.16
  164.6 1.6 copy.17

commit v4 on v2

v4 whole, which is shorter than its diff:
```python
import jax
import jax.numpy as jnp
from jax import lax
from jax.experimental import pallas as pl
from jax.experimental.pallas import tpu as pltpu
from jax.sharding import PartitionSpec as P

MESH = pl.DeviceIdType.MESH
KV = 512
GROUPS = 8
score_scale = 192.0 ** (-0.5)


D = 7168
norm_eps = 1e-06
A_COLS = 1024


def layer_kernel(
    length_ref, partner_ref, slot_ref, query_ref, cache_ref, up_ref, resid_ref, gain_ref,
    wo_ref, wg_ref, wu_ref, wd_ref, att_x, lay_x,
    query_buf, cache_buf, up_buf, lat_out, lat_in, wide, vals,
    wo, wg, wu, wd, resid_both, gain_own, gain_both,
    vb, c_out, c_in, cy_out, cy_in, xb, part_a, part_b, a1_in, a2, am_in, a_in, bm_in, b_in,
    b2_out, b2_in, b_keep, hb, g_out, g_in, gy_out, gy_in, resid_rows, turned,
    load_sem, up_sem, own_sem, l_s, l_r,
    w_l, w_s, w_r, v_s, v_r, c_s, c_r, x_s, x_r, a1_s, a1_r, a_s, a_r, b_s, b_r, b2_s, b2_r,
    h_s, h_r, g_s, g_r, o_s, o_r,
):
    g = lax.axis_index("dp")
    t = lax.axis_index("tp")
    c = lax.rem(t, 2)
    q = t // 2
    z = q // 2
    yh = lax.rem(q, 2)
    x = g // 2
    yl = lax.rem(g, 2)
    slots = query_ref.shape[0]
    heads = up_ref.shape[0]
    rows = GROUPS * slots
    feats = wo_ref.shape[0]
    ff = wg_ref.shape[1]
    both = 2 * feats
    b_half = ff - A_COLS
    b_cols = 2 * b_half
    half = rows // 2
    f32 = jnp.float32
    bf16 = jnp.bfloat16

    def other_group(k):
        return (lax.rem(g + k, GROUPS), t)

    def other_z(k):
        return (g, lax.rem(z + k, 4) * 4 + yh * 2 + c)

    def chip(zp):
        return (g, zp * 4 + yh * 2 + c)

    def other_x(k):
        return (lax.rem(x + k, 4) * 2 + yl, t)

    low_peer = (x * 2 + 1 - yl, t)
    y_peer = (g, z * 4 + (1 - yh) * 2 + c)
    sibling = (g, q * 2 + 1 - c)

    def remote(src, dst, send_sem, recv_sem, device):
        return pltpu.make_async_remote_copy(
            src_ref=src, dst_ref=dst, send_sem=send_sem, recv_sem=recv_sem,
            device_id=device, device_id_type=MESH,
        )

    def arrived(ref, sem):
        remote(ref, ref, sem, sem, sibling).wait_recv()

    def left(ref, sem):
        remote(ref, ref, sem, sem, sibling).wait_send()

    def order(i):
        return i + (i // 2) * (5 - 2 * i)

    def loads(r):
        return (
            pltpu.make_async_copy(query_ref.at[r], query_buf.at[r], load_sem.at[0, r]),
            pltpu.make_async_copy(cache_ref.at[r], cache_buf.at[r], load_sem.at[1, r]),
        )

    for r in range(slots):
        for copy in loads(r):
            copy.start()
    up_copy = pltpu.make_async_copy(up_ref, up_buf, up_sem)
    up_copy.start()
    barrier = pltpu.get_barrier_semaphore()
    greeted = [other_group(k) for k in range(1, GROUPS)]
    greeted += [other_z(k) for k in (1, 2, 3)] + [y_peer, sibling]
    for device in greeted:
        pl.semaphore_signal(barrier, inc=1, device_id=device, device_id_type=MESH)

    own_rows = pl.ds(pl.multiple_of(c * feats, feats), feats)
    gain_own[...] = jnp.transpose(
        jnp.broadcast_to(gain_ref[...].astype(f32), (128, feats)), (1, 0)
    ).astype(bf16)
    weights = (
        (wo_ref, wo), (resid_ref, resid_both), (gain_own, gain_both),
        (wg_ref, wg), (wu_ref, wu), (wd_ref, wd),
    )

    def start_weights():
        for i, (src, dst) in enumerate(weights):
            remote(src, dst.at[own_rows], w_s.at[i], w_r.at[i], sibling).start()
            pltpu.make_async_copy(src, dst.at[own_rows], w_l.at[i]).start()

    pl.semaphore_wait(barrier, len(greeted))

    upper = pl.ds(0, half)
    lower = pl.ds(half, half)

    def gather_start(buf, s, r):
        own_a = buf.at[q, upper]
        own_b = buf.at[q, lower]
        remote(own_a, own_a, s.at[0], r.at[0], y_peer).start()
        for k in (2, 1, 3):
            remote(own_b, own_b, s.at[k], r.at[k], other_z(k)).start()
        remote(own_b, own_b, s.at[10], r.at[10], y_peer).start()
        for k in (2, 1, 3):
            remote(own_a, own_a, s.at[3 + k], r.at[3 + k], other_z(k)).start()

    def forward_y(buf, s, r):
        block = buf.at[z * 2 + 1 - yh, upper]
        arrived(block, r.at[0])
        for k in (2, 1, 3):
            remote(block, block, s.at[6 + k], r.at[6 + k], other_z(k)).start()

    def forward_z(buf, s, r, k):
        block = buf.at[lax.rem(z + 4 - k, 4) * 2 + yh, lower]
        arrived(block, r.at[k])
        remote(block, block, s.at[10 + k], r.at[10 + k], y_peer).start()

    def project(buf, w, s, r, out, landed, out_s, out_r):
        forward_y(buf, s, r)
        forward_z(buf, s, r, 1)
        forward_z(buf, s, r, 3)

        def step(i, carry):
            k = jnp.where(i == 0, 0, 1 + lax.rem(i + 2 + x, 3))
            zp = lax.rem(z + 4 - k, 4)
            arrived(buf.at[0, lower], r.at[10 + k])

            @pl.when(k > 0)
            def _():
                arrived(buf.at[0, upper], r.at[3 + k])
                arrived(buf.at[0, upper], r.at[6 + k])

            left_rows = buf[pl.ds(2 * zp, 2)].reshape(2 * rows, buf.shape[2])
            product = lax.dot_general(
                left_rows, w[...], (((1,), (1,)), ((), ())), preferred_element_type=f32
            )
            out[pl.ds(2 * zp, 2)] = product.astype(bf16).reshape(2, rows, both)

            @pl.when(zp != x)
            def _():
                remote(
                    out.at[pl.ds(2 * zp, 2)], landed.at[x], out_s.at[zp], out_r.at[x],
                    (zp * 2 + yl, t),
                ).start()

            @pl.when(i == 0)
            def _():
                forward_z(buf, s, r, 2)

            return carry

        lax.fori_loop(0, 4, step, 0)

    def gathered_sum(out, landed, y_out, y_in, out_s, out_r):
        for k in (1, 3, 2):
            p = lax.rem(x + k, 4)
            arrived(landed.at[p], out_r.at[p])

        def over_x(j):
            total = out[2 * x + j].astype(f32)
            for k in (1, 3, 2):
                total += landed[lax.rem(x + k, 4), j].astype(f32)
            return total

        y_out[...] = over_x(1 - yl).astype(bf16)
        remote(y_out, y_in, out_s.at[4], out_r.at[4], low_peer).start()
        total = over_x(yl)
        arrived(y_in, out_r.at[4])
        return total + y_in[...].astype(f32)

    def finish_gather(buf, s):
        for i in range(14):
            left(buf.at[0, upper], s.at[i])

    def finish_sends(out, y_out, out_s):
        for k in (1, 2, 3):
            left(out.at[pl.ds(0, 2)], out_s.at[lax.rem(x + k, 4)])
        left(y_out, out_s.at[4])

    def with_sum(square_sum):
        high = square_sum.astype(bf16).astype(f32)
        lane = lax.broadcasted_iota(jnp.int32, (square_sum.shape[0], 128), 1)
        return jnp.where(
            lane == 0, high, jnp.where(lane == 1, square_sum - high, 0.0)
        ).astype(bf16)

    def send(k, r):
        p = lax.rem(g + k, GROUPS)
        return pltpu.make_async_remote_copy(
            src_ref=lat_out.at[pl.ds(r, 2), pl.ds(pl.multiple_of(p * heads, heads), heads)],
            dst_ref=lat_in.at[g, pl.ds(r, 2)],
            send_sem=l_s.at[k],
            recv_sem=l_r.at[g],
            device_id=(p, t),
            device_id_type=MESH,
        )

    def attend(r):
        for copy in loads(r):
            copy.wait()
        length = length_ref[g, r]
        cache = cache_buf[r]
        scores = lax.dot_general(
            query_buf[r], cache, (((0,), (0,)), ((), ())), preferred_element_type=jnp.float32
        )
        position = lax.broadcasted_iota(jnp.int32, scores.shape, 1)
        masked = jnp.where(position < length, scores * score_scale, -jnp.inf)
        largest = jnp.max(masked, axis=1, keepdims=True)
        expterm = jnp.exp(masked - largest)
        total = jnp.sum(expterm, axis=1, keepdims=True)
        weights = (expterm / total).astype(jnp.bfloat16)
        latent = lax.dot_general(
            weights, cache[:KV], (((1,), (1,)), ((), ())), preferred_element_type=jnp.float32
        )
        lat_out[r] = latent.astype(jnp.bfloat16)

    def pair(i, carry):
        attend(2 * i)
        attend(2 * i + 1)
        for k in (4, 3, 5, 2, 6, 1, 7):
            send(k, 2 * i).start()

        @pl.when(i == 0)
        def _():
            start_weights()

        return carry

    lax.fori_loop(0, slots // 2, pair, 0)
    own = pltpu.make_async_copy(
        lat_out.at[:, pl.ds(pl.multiple_of(g * heads, heads), heads)], lat_in.at[g], own_sem
    )
    own.start()
    own.wait()
    up_copy.wait()

    def widen(k, carry):
        s = lax.rem(g + k, GROUPS)

        @pl.when(k > 0)
        def _():
            pltpu.make_async_remote_copy(
                src_ref=lat_in.at[s], dst_ref=lat_in.at[s], send_sem=l_s.at[0],
                recv_sem=l_r.at[s], device_id=(s, t), device_id_type=MESH,
            ).wait_recv()

        step_rows = slots * heads
        block = lat_in[s].astype(jnp.float32).reshape(step_rows, KV)
        for lane in range(KV // 128):
            wide[lane, pl.ds(pl.multiple_of(s * step_rows, step_rows), step_rows)] = block[
                :, lane * 128 : (lane + 1) * 128
            ]
        return carry

    lax.fori_loop(0, GROUPS, widen, 0)
    count = GROUPS * slots
    for h in range(heads):
        head_rows = jnp.concatenate(
            [wide[lane, pl.ds(h, count, stride=heads), :] for lane in range(KV // 128)], axis=1
        )
        vals[:, h * 128 : (h + 1) * 128] = jnp.dot(
            head_rows.astype(jnp.bfloat16),
            up_buf[h],
            preferred_element_type=jnp.float32,
        ).astype(jnp.bfloat16)
    row = lax.broadcasted_iota(jnp.int32, (count, count), 0)
    column = lax.broadcasted_iota(jnp.int32, (count, count), 1)
    source = row
    for group in range(GROUPS):
        partner = partner_ref[group]
        own_row = group * slots + slot_ref[group]
        source = jnp.where(row == own_row, partner * slots + slot_ref[partner], source)
    place = jnp.where(column == source, 1.0, 0.0).astype(jnp.bfloat16)
    vb[q] = jnp.dot(place, vals[...], preferred_element_type=jnp.float32).astype(
        jnp.bfloat16
    )
    gather_start(vb, v_s, v_r)

    def weight_ready(i):
        src, dst = weights[i]
        pltpu.make_async_copy(src, dst.at[own_rows], w_l.at[i]).wait()
        arrived(dst.at[own_rows], w_r.at[i])

    for i in range(3):
        weight_ready(i)
    mine = pl.ds(pl.multiple_of(c * rows, rows), rows)
    turned[...] = resid_both[...].astype(f32)
    resid_rows[...] = jnp.transpose(turned[...], (1, 0))
    project(vb, wo, v_s, v_r, c_out, c_in, c_s, c_r)
    attn = gathered_sum(c_out, c_in, cy_out, cy_in, c_s, c_r)
    att_x[c] = attn.astype(bf16)
    remote(att_x.at[c], att_x.at[c], o_s.at[0], o_r.at[0], sibling).start()
    resid = resid_rows[mine] + attn
    resid_rows[mine] = resid
    gain = jnp.transpose(gain_both[...].astype(f32), (1, 0))[:1]
    xb[g, :, :both] = (resid * gain).astype(bf16)
    xb[g, :, both:] = with_sum(jnp.sum(resid * resid, axis=1, keepdims=True))
    remote(xb.at[g], xb.at[g], x_s.at[0], x_r.at[0], low_peer).start()
    for k in (1, 3, 2):
        remote(xb.at[g], xb.at[g], x_s.at[k], x_r.at[k], other_x(k)).start()
    low_block = xb.at[x * 2 + 1 - yl]
    arrived(low_block, x_r.at[0])
    for k in (1, 3, 2):
        remote(low_block, low_block, x_s.at[3 + k], x_r.at[3 + k], other_x(k)).start()
    for i in range(3, 6):
        weight_ready(i)

    def first_products(i, carry):
        k = order(i)
        xp = lax.rem(x + 4 - k, 4)

        @pl.when(k > 0)
        def _():
            arrived(xb.at[0], x_r.at[k])
            arrived(xb.at[0], x_r.at[3 + k])

        block = xb[pl.ds(2 * xp, 2)].reshape(2 * rows, both + 128)
        pair = pl.ds(2 * xp, 2)
        lhs = block[:, :both]

        def product(w, start, width):
            return jnp.dot(
                lhs, w[:, start : start + width], preferred_element_type=f32
            ).astype(bf16).reshape(2, rows, width)

        part_a[pair, :, :A_COLS] = product(wg, 0, A_COLS)
        part_a[pair, :, A_COLS:] = product(wu, 0, A_COLS)
        remote(
            part_a.at[2 * xp + 1 - yh], a1_in.at[xp], a1_s.at[xp], a1_r.at[xp], y_peer
        ).start()
        part_b[pair, :, :b_half] = product(wg, A_COLS, b_half)
        part_b[pair, :, b_half:b_cols] = product(wu, A_COLS, b_half)
        part_b[pair, :, b_cols:] = block[:, both:].reshape(2, rows, 128)
        role = lax.rem(xp + 4 - z, 4)

        @pl.when(role == 2)
        def _():
            for j in range(2):
                remote(
                    part_b.at[2 * xp + j], bm_in.at[j], b_s.at[j], b_r.at[j], other_z(1 + 2 * j)
                ).start()

        for j in range(2):

            @pl.when(role == 3 - 2 * j)
            def _():
                remote(
                    part_b.at[2 * xp + j], b_in.at[1 - j, j], b_s.at[2 + j], b_r.at[2 + j],
                    other_z(3 - 2 * j),
                ).start()

        return carry

    lax.fori_loop(0, 4, first_products, 0)
    halves = (upper, lower)

    def second_a(i, carry):
        xp = lax.rem(x + 4 - order(i), 4)
        arrived(a1_in.at[xp], a1_r.at[xp])
        a2[xp] = (part_a[2 * xp + yh].astype(f32) + a1_in[xp].astype(f32)).astype(bf16)
        role = lax.rem(xp + 4 - z, 4)

        @pl.when(role == 2)
        def _():
            for j in range(2):
                remote(
                    a2.at[xp, halves[j]], am_in.at[j], a_s.at[j], a_r.at[j], other_z(1 + 2 * j)
                ).start()

        for j in range(2):

            @pl.when(role == 3 - 2 * j)
            def _():
                remote(
                    a2.at[xp, halves[j]], a_in.at[1 - j, halves[j]], a_s.at[2 + j],
                    a_r.at[2 + j], other_z(3 - 2 * j),
                ).start()

        return carry

    def total_squares(block):
        return block[:, 0:1] + block[:, 1:2]

    def relay_b(j):
        block = 2 * lax.rem(z + 1 + 2 * j, 4) + j
        arrived(bm_in.at[j], b_r.at[j])
        total = part_b[block].astype(f32) + bm_in[j].astype(f32)
        part_b[block, :, :b_cols] = total[:, :b_cols].astype(bf16)
        part_b[block, :, b_cols:] = with_sum(total_squares(total[:, b_cols:]))
        remote(
            part_b.at[block], b_in.at[j, j], b_s.at[4 + j], b_r.at[4 + j], other_z(1 + 2 * j)
        ).start()

    def relay_a(j):
        block = lax.rem(z + 1 + 2 * j, 4)
        arrived(am_in.at[j], a_r.at[j])
        a2[block, halves[j]] = (
            a2[block, halves[j]].astype(f32) + am_in[j].astype(f32)
        ).astype(bf16)
        remote(
            a2.at[block, halves[j]], a_in.at[j, halves[j]], a_s.at[4 + j], a_r.at[4 + j],
            other_z(1 + 2 * j),
        ).start()

    lax.fori_loop(0, 1, second_a, 0)
    for j in range(2):
        relay_b(j)
    lax.fori_loop(1, 3, second_a, 0)
    for j in range(2):
        arrived(b_in.at[1 - j, j], b_r.at[2 + j])
        arrived(b_in.at[j, j], b_r.at[4 + j])

    def sum_b(j):
        return part_b[2 * z + j].astype(f32) + b_in[0, j].astype(f32) + b_in[1, j].astype(f32)

    away = sum_b(1 - yh)
    b2_out[:, :b_cols] = away[:, :b_cols].astype(bf16)
    b2_out[:, b_cols:] = with_sum(total_squares(away[:, b_cols:]))
    remote(b2_out, b2_in, b2_s.at[0], b2_r.at[0], y_peer).start()
    b_keep[...] = sum_b(yh)
    lax.fori_loop(3, 4, second_a, 0)
    for j in range(2):
        relay_a(j)
    arrived(b2_in, b2_r.at[0])

    def sum_b2(start, width):
        cols = slice(start, start + width)
        return b_keep[:, cols] + b2_in[:, cols].astype(f32)

    scale = lax.rsqrt(total_squares(sum_b2(b_cols, 128)) / D + norm_eps)

    def write_hidden(start, gate, upward):
        gate = gate * scale
        hb[q, :, start : start + gate.shape[1]] = (
            gate / (1.0 + jnp.exp(-gate)) * (upward * scale)
        ).astype(bf16)

    write_hidden(A_COLS, sum_b2(0, b_half), sum_b2(b_half, b_half))
    for j in range(2):
        arrived(a_in.at[1 - j, halves[j]], a_r.at[2 + j])
        arrived(a_in.at[j, halves[j]], a_r.at[4 + j])

    def sum_a(start):
        cols = slice(start, start + A_COLS)
        return (
            a2[z, :, cols].astype(f32) + a_in[0, :, cols].astype(f32)
            + a_in[1, :, cols].astype(f32)
        )

    write_hidden(0, sum_a(0), sum_a(A_COLS))
    gather_start(hb, h_s, h_r)
    project(hb, wd, h_s, h_r, g_out, g_in, g_s, g_r)
    down = gathered_sum(g_out, g_in, gy_out, gy_in, g_s, g_r)
    lay_x[c] = (resid_rows[mine] + down).astype(bf16)
    remote(lay_x.at[c], lay_x.at[c], o_s.at[1], o_r.at[1], sibling).start()
    arrived(att_x.at[1 - c], o_r.at[0])
    arrived(lay_x.at[1 - c], o_r.at[1])

    for k in range(1, GROUPS):
        left(lat_in.at[0], l_s.at[k])
    for i, (src, dst) in enumerate(weights):
        left(src, w_s.at[i])
    finish_gather(vb, v_s)
    finish_gather(hb, h_s)
    finish_sends(c_out, cy_out, c_s)
    finish_sends(g_out, gy_out, g_s)
    for k in range(7):
        left(xb.at[0], x_s.at[k])
    for i in range(4):
        left(part_a.at[0], a1_s.at[i])
    for i in range(6):
        left(part_b.at[0], b_s.at[i])
        left(a2.at[0, upper], a_s.at[i])
    left(b2_out, b2_s.at[0])
    left(att_x.at[0], o_s.at[0])
    left(lay_x.at[0], o_s.at[1])


def finish_kernel(att_ref, lay_ref, attended_ref, out_ref, turned):
    feats = attended_ref.shape[0]
    c = lax.rem(lax.axis_index("tp"), 2)
    own = pl.ds(pl.multiple_of(c * feats, feats), feats)
    for exchange, target in ((att_ref, attended_ref), (lay_ref, out_ref)):
        stacked = exchange[...].reshape(-1, 2 * feats).astype(jnp.float32)
        turned[...] = jnp.transpose(stacked, (1, 0))
        target[...] = turned[own].astype(target.dtype)


def run_layer(
    lengths, dest_group, moved_slot, queries, kv_cache, residual_in, norm_gain, up_value, out_proj,
    gate_proj, up_proj, down_proj,
):
    slots, all_heads, _ = queries.shape
    heads = up_value.shape[0]
    rows, width = GROUPS * slots, heads * 128
    queries = jnp.swapaxes(queries, 1, 2)
    kv_cache = jnp.swapaxes(kv_cache, 1, 2)
    total_rows, feats = residual_in.shape
    ff = gate_proj.shape[1]
    both = 2 * feats
    a_cols, b_cols = 2 * A_COLS, 2 * (ff - A_COLS) + 128
    f32, bf16 = jnp.float32, jnp.bfloat16
    vmem = pl.BlockSpec(memory_space=pltpu.VMEM)
    smem = pl.BlockSpec(memory_space=pltpu.SMEM)
    hbm = pl.BlockSpec(memory_space=pl.ANY)
    dma = pltpu.SemaphoreType.DMA
    block = jax.ShapeDtypeStruct((2, rows, both), bf16)
    turned = jax.ShapeDtypeStruct((feats, total_rows), bf16)
    att_x, lay_x = pl.pallas_call(
        layer_kernel,
        name="layer",
        out_shape=(block, block),
        in_specs=[smem, smem, smem, hbm, hbm, hbm, hbm, vmem, hbm, hbm, hbm, hbm],
        out_specs=(vmem, vmem),
        scratch_shapes=[
            pltpu.VMEM(queries.shape, bf16),
            pltpu.VMEM(kv_cache.shape, bf16),
            pltpu.VMEM(up_value.shape, bf16),
            pltpu.VMEM((slots, all_heads, KV), bf16),
            pltpu.VMEM((GROUPS, slots, heads, KV), bf16),
            pltpu.VMEM((KV // 128, rows * heads, 128), f32),
            pltpu.VMEM((rows, width), bf16),
            pltpu.VMEM((both, width), bf16),
            pltpu.VMEM((both, ff), bf16),
            pltpu.VMEM((both, ff), bf16),
            pltpu.VMEM((both, ff), bf16),
            pltpu.VMEM((both, total_rows), bf16),
            pltpu.VMEM((feats, 128), bf16),
            pltpu.VMEM((both, 128), bf16),
            pltpu.VMEM((8, rows, width), bf16),
            pltpu.VMEM((8, rows, both), bf16),
            pltpu.VMEM((4, 2, rows, both), bf16),
            pltpu.VMEM((rows, both), bf16),
            pltpu.VMEM((rows, both), bf16),
            pltpu.VMEM((8, rows, both + 128), bf16),
            pltpu.VMEM((8, rows, a_cols), bf16),
            pltpu.VMEM((8, rows, b_cols), bf16),
            pltpu.VMEM((4, rows, a_cols), bf16),
            pltpu.VMEM((4, rows, a_cols), bf16),
            pltpu.VMEM((2, rows // 2, a_cols), bf16),
            pltpu.VMEM((2, rows, a_cols), bf16),
            pltpu.VMEM((2, rows, b_cols), bf16),
            pltpu.VMEM((2, 2, rows, b_cols), bf16),
            pltpu.VMEM((rows, b_cols), bf16),
            pltpu.VMEM((rows, b_cols), bf16),
            pltpu.VMEM((rows, b_cols), f32),
            pltpu.VMEM((8, rows, ff), bf16),
            pltpu.VMEM((8, rows, both), bf16),
            pltpu.VMEM((4, 2, rows, both), bf16),
            pltpu.VMEM((rows, both), bf16),
            pltpu.VMEM((rows, both), bf16),
            pltpu.VMEM((total_rows, both), f32),
            pltpu.VMEM((both, total_rows), f32),
            dma((2, slots)), dma, dma, dma((8,)), dma((8,)),
            dma((6,)), dma((6,)), dma((6,)), dma((14,)), dma((14,)),
            dma((5,)), dma((5,)), dma((7,)), dma((7,)),
            dma((4,)), dma((4,)), dma((6,)), dma((6,)), dma((6,)), dma((6,)), dma((1,)), dma((1,)),
            dma((14,)), dma((14,)), dma((5,)), dma((5,)), dma((2,)), dma((2,)),
        ],
        compiler_params=pltpu.CompilerParams(
            collective_id=0, has_side_effects=True, vmem_limit_bytes=62 << 20
        ),
        cost_estimate=pl.CostEstimate(
            flops=2 * total_rows * 8 * feats * (width + 3 * ff), bytes_accessed=30 << 20,
            transcendentals=1 << 20,
        ),
    )(
        lengths[:, 0, :], dest_group[:, 0], moved_slot[:, 0], queries, kv_cache, up_value,
        jnp.swapaxes(residual_in, 0, 1), norm_gain[None, :], jnp.swapaxes(out_proj, 0, 1),
        gate_proj, up_proj, jnp.swapaxes(down_proj, 0, 1),
    )
    attended, layer_out = pl.pallas_call(
        finish_kernel,
        name="finish",
        out_shape=(turned, turned),
        in_specs=[vmem, vmem],
        out_specs=(vmem, vmem),
        scratch_shapes=[pltpu.VMEM((both, total_rows), f32)],
    )(att_x, lay_x)
    return jnp.swapaxes(attended, 0, 1), jnp.swapaxes(layer_out, 0, 1)


def shards(
    queries,
    kv_cache,
    lengths,
    dest_group,
    moved_slot,
    residual_in,
    norm_gain,
    up_value,
    out_proj,
    gate_proj,
    up_proj,
    down_proj,
):
    return run_layer(
        lengths, dest_group, moved_slot, queries, kv_cache, residual_in, norm_gain, up_value,
        out_proj, gate_proj, up_proj, down_proj,
    )


def solution(mesh):
    return jax.shard_map(
        shards,
        mesh=mesh,
        in_specs=(
            P(("dp", "tp"), None, None),
            P(("dp", "tp"), None, None),
            P(None, "tp", None),
            P(None, "tp"),
            P(None, "tp"),
            P("dp", "tp"),
            P("tp"),
            P("dp", None, None),
            P("dp", "tp"),
            P("tp", "dp"),
            P("tp", "dp"),
            P("dp", "tp"),
        ),
        out_specs=(P("dp", "tp"), P("dp", "tp")),
        check_vma=False,
    )
```

time: 388 us -> 151 us (0.39); the launches traced: 382 us -> 151 us
  waiting for transfers between devices: 236 us -> 0 us
  Pallas kernels: 21 us -> 149 us
  blocking collectives: 80.8 us -> 0 us
  matrix products: 16 us -> 0 us
  between operations: 14.5 us -> 0.64 us
  other arithmetic: 7.73 us -> 0 us
  local copies, waits for them, and re-layouts: 5.88 us -> 1.26 us
    pallas_call x1 -> x2, Pallas kernels: 21 us -> 149 us  [the longest x1 147 us: run_layer(): pl.pallas_call(layer_kernel, name='layer', out_shape=(block, block), in_s...]
    all_gather x2 -> x0, waiting for transfers between devices: 117 us -> none  [the longest x1 58.4 us: shards(): lax.all_gather(values, 'tp', axis=0, tiled=True)]
    unnamed x7 -> x0, waiting for transfers between devices: 62.7 us -> none
    reduce_scatter x1 -> x0, waiting for transfers between devices: 56.4 us -> none  [shards(): lax.psum_scatter(partial_gate.astype(jnp.bfloat16), 'tp', scatter_dimensi...]
    unnamed x1 -> x0, blocking collectives: 46.4 us -> none
    all_gather x2 -> x0, blocking collectives: 34.4 us -> none  [the longest x1 23.1 us: shards(): block_rows = lax.all_gather(scaled, 'dp', axis=0, tiled=True)]
    dot_general x4 -> x0, matrix products: 16 us -> none  [the longest x1 5.34 us: shards(): jnp.dot(block_rows, down_proj, preferred_element_type=jnp.float32)]
    unnamed x17 -> x0, local copies, waits for them, and re-layouts: 5.88 us -> none
  transfers between devices with their start and end apart: 5 -> 0, of which waited for: 5 -> 0; matrix products, arithmetic and copies ran while one was open for 0% -> 0% of each run, Pallas kernels for 0% -> 0%
where the time goes in v4:
time: 151 us
  Pallas kernels  149 us (99%)
    pallas_call x1, Pallas kernels, run_layer(): pl.pallas_call(layer_kernel, name='layer', out_shape=(block, block), in_s...  147 us

profile of v4, /device:TPU:3, one launch (start us, length us, event | category | flops | bytes accessed | tf_op | source)
XLA Modules:
  0.0 150.6 jit_solution(8005316495087617487)
XLA Ops:
  0.6 1.3 broadcast_in_dim.3.gain_ref
  1.9 146.7 %layer.1 = (bf16[2,64,896]{2,1,0:T(8,128)(2,1)}, bf16[2,64,896]{2,1,0:T(8,128)(2,1)}) custom-call(s32[8,8]{1,0:T(8,128)} %bitcast.17, s32[8]{0:T(128)} %bitcast.18, s32[8]{0:T(128)} %bitcast.19, bf16[8,576,128]{2,1,0:T(8,128)(2,1)} %bitcast.13, bf16[8,576,1024]{2,1,0:T(8,128)(2,1)} %bitcast.10, bf16[16,512,128]{2,1,0:T(8,128)(2,1)} %up_ref.1, ...), custom_call_target="tpu_custom_call" | custom-call | flops 8220835840 | bytes 31457280 | tf_op jit(solution)/shard_map/layer/pallas_call | solution.py:529
  148.6 2.0 %finish.1 = (bf16[448,128]{1,0:T(8,128)(2,1)}, bf16[448,128]{1,0:T(8,128)(2,1)}) custom-call(bf16[2,64,896]{2,1,0:T(8,128)(2,1)} %get-tuple-element.6.att_ref, bf16[2,64,896]{2,1,0:T(8,128)(2,1)} %get-tuple-element.7.lay_ref), custom_call_target="tpu_custom_call" | custom-call | tf_op jit(solution)/shard_map/finish/pallas_call | solution.py:592

commit v5 on v4

--- a/solution.py
+++ b/solution.py
@@ -8,7 +8,7 @@
 MESH = pl.DeviceIdType.MESH
 KV = 512
 GROUPS = 8
-score_scale = 192.0 ** (-0.5)
+exponent_scale = 192.0 ** (-0.5) * 1.4426950408889634
 
 
 D = 7168
@@ -114,42 +114,86 @@
     upper = pl.ds(0, half)
     lower = pl.ds(half, half)
 
-    def gather_start(buf, s, r):
-        own_a = buf.at[q, upper]
-        own_b = buf.at[q, lower]
-        remote(own_a, own_a, s.at[0], r.at[0], y_peer).start()
-        for k in (2, 1, 3):
-            remote(own_b, own_b, s.at[k], r.at[k], other_z(k)).start()
-        remote(own_b, own_b, s.at[10], r.at[10], y_peer).start()
-        for k in (2, 1, 3):
-            remote(own_a, own_a, s.at[3 + k], r.at[3 + k], other_z(k)).start()
-
-    def forward_y(buf, s, r):
-        block = buf.at[z * 2 + 1 - yh, upper]
+    quarter = half // 2
+    first = pl.ds(0, quarter)
+    second = pl.ds(quarter, quarter)
+    third = pl.ds(half, quarter)
+    fourth = pl.ds(half + quarter, quarter)
+    over_z = (other_z, y_peer, lambda k: lax.rem(z + 4 - k, 4) * 2 + yh,
+              lambda k: lax.rem(z + 4 - k, 4) * 2 + 1 - yh)
+    over_x = (other_x, low_peer, lambda k: lax.rem(x + 4 - k, 4) * 2 + yl,
+              lambda k: lax.rem(x + 4 - k, 4) * 2 + 1 - yl)
+
+    def push(ref, s, r, i, device):
+        remote(ref, ref, s.at[i], r.at[i], device).start()
+
+    def gather_start(buf, s, r, ways):
+        ring, peer, near, far = ways
+        own = buf.at[near(0)]
+        push(own.at[upper], s, r, 0, peer)
+        push(own.at[lower], s, r, 1, ring(1))
+        push(own.at[lower], s, r, 2, ring(3))
+        push(own.at[upper], s, r, 3, ring(1))
+        push(own.at[upper], s, r, 4, ring(3))
+        push(own.at[lower], s, r, 5, peer)
+
+    def gather_relay(buf, s, r, ways):
+        ring, peer, near, far = ways
+        block = buf.at[far(0), upper]
         arrived(block, r.at[0])
-        for k in (2, 1, 3):
-            remote(block, block, s.at[6 + k], r.at[6 + k], other_z(k)).start()
-
-    def forward_z(buf, s, r, k):
-        block = buf.at[lax.rem(z + 4 - k, 4) * 2 + yh, lower]
-        arrived(block, r.at[k])
-        remote(block, block, s.at[10 + k], r.at[10 + k], y_peer).start()
+        push(block, s, r, 6, ring(1))
+        push(block, s, r, 7, ring(3))
+        arrived(block, r.at[1])
+        push(buf.at[near(1), third], s, r, 8, ring(1))
+        push(buf.at[near(1), lower], s, r, 9, peer)
+        arrived(block, r.at[2])
+        push(buf.at[near(3), fourth], s, r, 10, ring(3))
+        push(buf.at[near(3), lower], s, r, 11, peer)
+        arrived(block, r.at[3])
+        push(buf.at[near(1), first], s, r, 12, ring(1))
+        arrived(block, r.at[4])
+        push(buf.at[near(3), second], s, r, 13, ring(3))
+
+    def gather_step(buf, s, r, ways, i):
+        ring, peer, near, far = ways
+        block = buf.at[far(0), upper]
+        piece = buf.at[far(0), first]
+
+        @pl.when(i == 0)
+        def _():
+            arrived(block, r.at[5])
+
+        @pl.when(i == 1)
+        def _():
+            arrived(block, r.at[6])
+            push(buf.at[far(1), first], s, r, 14, ring(1))
+            arrived(block, r.at[7])
+            push(buf.at[far(3), second], s, r, 15, ring(3))
+            arrived(piece, r.at[8])
+            push(buf.at[near(2), third], s, r, 16, peer)
+            arrived(piece, r.at[10])
+            push(buf.at[near(2), fourth], s, r, 17, peer)
+            arrived(block, r.at[9])
+
+        @pl.when(i == 2)
+        def _():
+            arrived(block, r.at[11])
+
+        @pl.when(i == 3)
+        def _():
+            for j in range(12, 18):
+                arrived(piece, r.at[j])
+
+    def finish_gather(buf, s):
+        for i in range(18):
+            left(buf.at[0, upper if i in (0, 1, 2, 3, 4, 5, 6, 7, 9, 11) else first], s.at[i])
 
     def project(buf, w, s, r, out, landed, out_s, out_r):
-        forward_y(buf, s, r)
-        forward_z(buf, s, r, 1)
-        forward_z(buf, s, r, 3)
+        gather_relay(buf, s, r, over_z)
 
         def step(i, carry):
-            k = jnp.where(i == 0, 0, 1 + lax.rem(i + 2 + x, 3))
-            zp = lax.rem(z + 4 - k, 4)
-            arrived(buf.at[0, lower], r.at[10 + k])
-
-            @pl.when(k > 0)
-            def _():
-                arrived(buf.at[0, upper], r.at[3 + k])
-                arrived(buf.at[0, upper], r.at[6 + k])
-
+            zp = lax.rem(z + 4 - order(i), 4)
+            gather_step(buf, s, r, over_z, i)
             left_rows = buf[pl.ds(2 * zp, 2)].reshape(2 * rows, buf.shape[2])
             product = lax.dot_general(
                 left_rows, w[...], (((1,), (1,)), ((), ())), preferred_element_type=f32
@@ -163,10 +207,6 @@
                     (zp * 2 + yl, t),
                 ).start()
 
-            @pl.when(i == 0)
-            def _():
-                forward_z(buf, s, r, 2)
-
             return carry
 
         lax.fori_loop(0, 4, step, 0)
@@ -187,10 +227,6 @@
         total = over_x(yl)
         arrived(y_in, out_r.at[4])
         return total + y_in[...].astype(f32)
-
-    def finish_gather(buf, s):
-        for i in range(14):
-            left(buf.at[0, upper], s.at[i])
 
     def finish_sends(out, y_out, out_s):
         for k in (1, 2, 3):
@@ -224,15 +260,15 @@
             query_buf[r], cache, (((0,), (0,)), ((), ())), preferred_element_type=jnp.float32
         )
         position = lax.broadcasted_iota(jnp.int32, scores.shape, 1)
-        masked = jnp.where(position < length, scores * score_scale, -jnp.inf)
+        masked = jnp.where(position < length, scores, -jnp.inf)
         largest = jnp.max(masked, axis=1, keepdims=True)
-        expterm = jnp.exp(masked - largest)
+        expterm = jnp.exp2((masked - largest) * exponent_scale)
         total = jnp.sum(expterm, axis=1, keepdims=True)
-        weights = (expterm / total).astype(jnp.bfloat16)
         latent = lax.dot_general(
-            weights, cache[:KV], (((1,), (1,)), ((), ())), preferred_element_type=jnp.float32
+            expterm.astype(jnp.bfloat16), cache[:KV], (((1,), (1,)), ((), ())),
+            preferred_element_type=jnp.float32,
         )
-        lat_out[r] = latent.astype(jnp.bfloat16)
+        lat_out[r] = (latent * (1.0 / total)).astype(jnp.bfloat16)
 
     def pair(i, carry):
         attend(2 * i)
@@ -294,7 +330,7 @@
     vb[q] = jnp.dot(place, vals[...], preferred_element_type=jnp.float32).astype(
         jnp.bfloat16
     )
-    gather_start(vb, v_s, v_r)
+    gather_start(vb, v_s, v_r, over_z)
 
     def weight_ready(i):
         src, dst = weights[i]
@@ -315,25 +351,15 @@
     gain = jnp.transpose(gain_both[...].astype(f32), (1, 0))[:1]
     xb[g, :, :both] = (resid * gain).astype(bf16)
     xb[g, :, both:] = with_sum(jnp.sum(resid * resid, axis=1, keepdims=True))
-    remote(xb.at[g], xb.at[g], x_s.at[0], x_r.at[0], low_peer).start()
-    for k in (1, 3, 2):
-        remote(xb.at[g], xb.at[g], x_s.at[k], x_r.at[k], other_x(k)).start()
-    low_block = xb.at[x * 2 + 1 - yl]
-    arrived(low_block, x_r.at[0])
-    for k in (1, 3, 2):
-        remote(low_block, low_block, x_s.at[3 + k], x_r.at[3 + k], other_x(k)).start()
+    gather_start(xb, x_s, x_r, over_x)
     for i in range(3, 6):
         weight_ready(i)
 
+    gather_relay(xb, x_s, x_r, over_x)
+
     def first_products(i, carry):
-        k = order(i)
-        xp = lax.rem(x + 4 - k, 4)
-
-        @pl.when(k > 0)
-        def _():
-            arrived(xb.at[0], x_r.at[k])
-            arrived(xb.at[0], x_r.at[3 + k])
-
+        xp = lax.rem(x + 4 - order(i), 4)
+        gather_step(xb, x_s, x_r, over_x, i)
         block = xb[pl.ds(2 * xp, 2)].reshape(2 * rows, both + 128)
         pair = pl.ds(2 * xp, 2)
         lhs = block[:, :both]
@@ -468,7 +494,7 @@
         )
 
     write_hidden(0, sum_a(0), sum_a(A_COLS))
-    gather_start(hb, h_s, h_r)
+    gather_start(hb, h_s, h_r, over_z)
     project(hb, wd, h_s, h_r, g_out, g_in, g_s, g_r)
     down = gathered_sum(g_out, g_in, gy_out, gy_in, g_s, g_r)
     lay_x[c] = (resid_rows[mine] + down).astype(bf16)
@@ -484,8 +510,7 @@
     finish_gather(hb, h_s)
     finish_sends(c_out, cy_out, c_s)
     finish_sends(g_out, gy_out, g_s)
-    for k in range(7):
-        left(xb.at[0], x_s.at[k])
+    finish_gather(xb, x_s)
     for i in range(4):
         left(part_a.at[0], a1_s.at[i])
     for i in range(6):
@@ -572,10 +597,10 @@
             pltpu.VMEM((total_rows, both), f32),
             pltpu.VMEM((both, total_rows), f32),
             dma((2, slots)), dma, dma, dma((8,)), dma((8,)),
-            dma((6,)), dma((6,)), dma((6,)), dma((14,)), dma((14,)),
-            dma((5,)), dma((5,)), dma((7,)), dma((7,)),
+            dma((6,)), dma((6,)), dma((6,)), dma((18,)), dma((18,)),
+            dma((5,)), dma((5,)), dma((18,)), dma((18,)),
             dma((4,)), dma((4,)), dma((6,)), dma((6,)), dma((6,)), dma((6,)), dma((1,)), dma((1,)),
-            dma((14,)), dma((14,)), dma((5,)), dma((5,)), dma((2,)), dma((2,)),
+            dma((18,)), dma((18,)), dma((5,)), dma((5,)), dma((2,)), dma((2,)),
         ],
         compiler_params=pltpu.CompilerParams(
             collective_id=0, has_side_effects=True, vmem_limit_bytes=62 << 20
@@ -586,7 +611,7 @@
         ),
     )(
         lengths[:, 0, :], dest_group[:, 0], moved_slot[:, 0], queries, kv_cache, up_value,
-        jnp.swapaxes(residual_in, 0, 1), norm_gain[None, :], jnp.swapaxes(out_proj, 0, 1),
+        jnp.swapaxes(residual_in, 0, 1), norm_gain, jnp.swapaxes(out_proj, 0, 1),
         gate_proj, up_proj, jnp.swapaxes(down_proj, 0, 1),
     )
     attended, layer_out = pl.pallas_call(

time: 151 us -> 137 us (0.907); the launches traced: 151 us -> 134 us
  Pallas kernels: 149 us -> 134 us
    pallas_call x1, Pallas kernels: 147 us -> 132 us  [run_layer(): pl.pallas_call(layer_kernel, name='layer', out_shape=(block, block), in_s...]
where the time goes in v5:
time: 137 us; the launch traced here: 134 us
  Pallas kernels  134 us (98%)
    pallas_call x1, Pallas kernels, run_layer(): pl.pallas_call(layer_kernel, name='layer', out_shape=(block, block), in_s...  132 us

profile of v5, /device:TPU:3, one launch (start us, length us, event | category | flops | bytes accessed | tf_op | source)
XLA Modules:
  0.0 134.5 jit_solution(2154787235013655806)
XLA Ops:
  0.6 131.9 %layer.1 = (bf16[2,64,896]{2,1,0:T(8,128)(2,1)}, bf16[2,64,896]{2,1,0:T(8,128)(2,1)}) custom-call(s32[8,8]{1,0:T(8,128)} %bitcast.17, s32[8]{0:T(128)} %bitcast.18, s32[8]{0:T(128)} %bitcast.19, bf16[8,576,128]{2,1,0:T(8,128)(2,1)} %bitcast.13, bf16[8,576,1024]{2,1,0:T(8,128)(2,1)} %bitcast.10, bf16[16,512,128]{2,1,0:T(8,128)(2,1)} %up_ref.1, ...), custom_call_target="tpu_custom_call" | custom-call | flops 8220835840 | bytes 31457280 | tf_op jit(solution)/shard_map/layer/pallas_call | solution.py:554
  132.5 2.0 %finish.1 = (bf16[448,128]{1,0:T(8,128)(2,1)}, bf16[448,128]{1,0:T(8,128)(2,1)}) custom-call(bf16[2,64,896]{2,1,0:T(8,128)(2,1)} %get-tuple-element.6.att_ref, bf16[2,64,896]{2,1,0:T(8,128)(2,1)} %get-tuple-element.7.lay_ref), custom_call_target="tpu_custom_call" | custom-call | tf_op jit(solution)/shard_map/finish/pallas_call | solution.py:617

commit v6 on v5

--- a/solution.py
+++ b/solution.py
@@ -13,7 +13,7 @@
 
 D = 7168
 norm_eps = 1e-06
-A_COLS = 1024
+A_COLS = 1152
 
 
 def layer_kernel(
@@ -21,8 +21,8 @@
     wo_ref, wg_ref, wu_ref, wd_ref, att_x, lay_x,
     query_buf, cache_buf, up_buf, lat_out, lat_in, wide, vals,
     wo, wg, wu, wd, resid_both, gain_own, gain_both,
-    vb, c_out, c_in, cy_out, cy_in, xb, part_a, part_b, a1_in, a2, am_in, a_in, bm_in, b_in,
-    b2_out, b2_in, b_keep, hb, g_out, g_in, gy_out, gy_in, resid_rows, turned,
+    vb, c_out, c_in, cy_out, cy_in, cl_in, xb, part_a, part_b, a1_in, a2, am_in, a_in, bm_in, b_in,
+    b2_out, b2_in, b_keep, hb, g_out, g_in, gy_out, gy_in, gl_in, summed, resid_rows, gain_row, turned,
     load_sem, up_sem, own_sem, l_s, l_r,
     w_l, w_s, w_r, v_s, v_r, c_s, c_r, x_s, x_r, a1_s, a1_r, a_s, a_r, b_s, b_r, b2_s, b2_r,
     h_s, h_r, g_s, g_r, o_s, o_r,
@@ -109,8 +109,6 @@
             remote(src, dst.at[own_rows], w_s.at[i], w_r.at[i], sibling).start()
             pltpu.make_async_copy(src, dst.at[own_rows], w_l.at[i]).start()
 
-    pl.semaphore_wait(barrier, len(greeted))
-
     upper = pl.ds(0, half)
     lower = pl.ds(half, half)
 
@@ -149,6 +147,10 @@
         arrived(block, r.at[2])
         push(buf.at[near(3), fourth], s, r, 10, ring(3))
         push(buf.at[near(3), lower], s, r, 11, peer)
+
+    def gather_more(buf, s, r, ways):
+        ring, peer, near, far = ways
+        block = buf.at[far(0), upper]
         arrived(block, r.at[3])
         push(buf.at[near(1), first], s, r, 12, ring(1))
         arrived(block, r.at[4])
@@ -165,6 +167,7 @@
 
         @pl.when(i == 1)
         def _():
+            gather_more(buf, s, r, ways)
             arrived(block, r.at[6])
             push(buf.at[far(1), first], s, r, 14, ring(1))
             arrived(block, r.at[7])
@@ -188,7 +191,9 @@
         for i in range(18):
             left(buf.at[0, upper if i in (0, 1, 2, 3, 4, 5, 6, 7, 9, 11) else first], s.at[i])
 
-    def project(buf, w, s, r, out, landed, out_s, out_r):
+    last = lax.rem(z + 2, 4)
+
+    def project(buf, w, s, r, out, landed, late_in, out_s, out_r):
         gather_relay(buf, s, r, over_z)
 
         def step(i, carry):
@@ -200,7 +205,7 @@
             )
             out[pl.ds(2 * zp, 2)] = product.astype(bf16).reshape(2, rows, both)
 
-            @pl.when(zp != x)
+            @pl.when((zp != x) & (i < 3))
             def _():
                 remote(
                     out.at[pl.ds(2 * zp, 2)], landed.at[x], out_s.at[zp], out_r.at[x],
@@ -210,28 +215,62 @@
             return carry
 
         lax.fori_loop(0, 4, step, 0)
+        there = out.at[2 * last + 1 - yl]
+        remote(there, late_in, out_s.at[5], out_r.at[5], low_peer).start()
+        arrived(late_in, out_r.at[5])
+        here = 2 * last + yl
+        out[here] = (out[here].astype(f32) + late_in[...].astype(f32)).astype(bf16)
+
+        @pl.when(last != x)
+        def _():
+            remote(
+                out.at[here], landed.at[x, yl], out_s.at[last], out_r.at[x], (last * 2 + yl, t)
+            ).start()
 
     def gathered_sum(out, landed, y_out, y_in, out_s, out_r):
-        for k in (1, 3, 2):
-            p = lax.rem(x + k, 4)
-            arrived(landed.at[p], out_r.at[p])
-
         def over_x(j):
             total = out[2 * x + j].astype(f32)
             for k in (1, 3, 2):
                 total += landed[lax.rem(x + k, 4), j].astype(f32)
             return total
 
-        y_out[...] = over_x(1 - yl).astype(bf16)
-        remote(y_out, y_in, out_s.at[4], out_r.at[4], low_peer).start()
-        total = over_x(yl)
-        arrived(y_in, out_r.at[4])
-        return total + y_in[...].astype(f32)
+        @pl.when(last != x)
+        def _():
+            for k in (1, 3, 2):
+                p = lax.rem(x + k, 4)
+                arrived(landed.at[p], out_r.at[p])
+            y_out[...] = over_x(1 - yl).astype(bf16)
+            remote(y_out, y_in, out_s.at[4], out_r.at[4], low_peer).start()
+            total = over_x(yl)
+            arrived(y_in, out_r.at[4])
+            summed[...] = total + y_in[...].astype(f32)
+
+        @pl.when(last == x)
+        def _():
+            for k in (1, 3, 2):
+                p = lax.rem(x + k, 4)
+                arrived(landed.at[p, yl], out_r.at[p])
+            summed[...] = over_x(yl)
+
+        return summed[...]
 
     def finish_sends(out, y_out, out_s):
         for k in (1, 2, 3):
-            left(out.at[pl.ds(0, 2)], out_s.at[lax.rem(x + k, 4)])
-        left(y_out, out_s.at[4])
+            p = lax.rem(x + k, 4)
+
+            @pl.when(p != last)
+            def _():
+                left(out.at[pl.ds(0, 2)], out_s.at[p])
+
+            @pl.when(p == last)
+            def _():
+                left(out.at[0], out_s.at[p])
+
+        @pl.when(last != x)
+        def _():
+            left(y_out, out_s.at[4])
+
+        left(out.at[0], out_s.at[5])
 
     def with_sum(square_sum):
         high = square_sum.astype(bf16).astype(f32)
@@ -275,14 +314,15 @@
         attend(2 * i + 1)
         for k in (4, 3, 5, 2, 6, 1, 7):
             send(k, 2 * i).start()
-
-        @pl.when(i == 0)
-        def _():
-            start_weights()
-
         return carry
 
-    lax.fori_loop(0, slots // 2, pair, 0)
+    attend(0)
+    attend(1)
+    pl.semaphore_wait(barrier, len(greeted))
+    for k in (4, 3, 5, 2, 6, 1, 7):
+        send(k, 0).start()
+    lax.fori_loop(1, slots // 2, pair, 0)
+    start_weights()
     own = pltpu.make_async_copy(
         lat_out.at[:, pl.ds(pl.multiple_of(g * heads, heads), heads)], lat_in.at[g], own_sem
     )
@@ -342,14 +382,14 @@
     mine = pl.ds(pl.multiple_of(c * rows, rows), rows)
     turned[...] = resid_both[...].astype(f32)
     resid_rows[...] = jnp.transpose(turned[...], (1, 0))
-    project(vb, wo, v_s, v_r, c_out, c_in, c_s, c_r)
+    gain_row[...] = jnp.transpose(gain_both[...].astype(f32), (1, 0))[:1]
+    project(vb, wo, v_s, v_r, c_out, c_in, cl_in, c_s, c_r)
     attn = gathered_sum(c_out, c_in, cy_out, cy_in, c_s, c_r)
     att_x[c] = attn.astype(bf16)
     remote(att_x.at[c], att_x.at[c], o_s.at[0], o_r.at[0], sibling).start()
     resid = resid_rows[mine] + attn
     resid_rows[mine] = resid
-    gain = jnp.transpose(gain_both[...].astype(f32), (1, 0))[:1]
-    xb[g, :, :both] = (resid * gain).astype(bf16)
+    xb[g, :, :both] = (resid * gain_row[...]).astype(bf16)
     xb[g, :, both:] = with_sum(jnp.sum(resid * resid, axis=1, keepdims=True))
     gather_start(xb, x_s, x_r, over_x)
     for i in range(3, 6):
@@ -495,7 +535,7 @@
 
     write_hidden(0, sum_a(0), sum_a(A_COLS))
     gather_start(hb, h_s, h_r, over_z)
-    project(hb, wd, h_s, h_r, g_out, g_in, g_s, g_r)
+    project(hb, wd, h_s, h_r, g_out, g_in, gl_in, g_s, g_r)
     down = gathered_sum(g_out, g_in, gy_out, gy_in, g_s, g_r)
     lay_x[c] = (resid_rows[mine] + down).astype(bf16)
     remote(lay_x.at[c], lay_x.at[c], o_s.at[1], o_r.at[1], sibling).start()
@@ -577,6 +617,7 @@
             pltpu.VMEM((4, 2, rows, both), bf16),
             pltpu.VMEM((rows, both), bf16),
             pltpu.VMEM((rows, both), bf16),
+            pltpu.VMEM((rows, both), bf16),
             pltpu.VMEM((8, rows, both + 128), bf16),
             pltpu.VMEM((8, rows, a_cols), bf16),
             pltpu.VMEM((8, rows, b_cols), bf16),
@@ -594,13 +635,16 @@
             pltpu.VMEM((4, 2, rows, both), bf16),
             pltpu.VMEM((rows, both), bf16),
             pltpu.VMEM((rows, both), bf16),
+            pltpu.VMEM((rows, both), bf16),
+            pltpu.VMEM((rows, both), f32),
             pltpu.VMEM((total_rows, both), f32),
+            pltpu.VMEM((1, both), f32),
             pltpu.VMEM((both, total_rows), f32),
             dma((2, slots)), dma, dma, dma((8,)), dma((8,)),
             dma((6,)), dma((6,)), dma((6,)), dma((18,)), dma((18,)),
-            dma((5,)), dma((5,)), dma((18,)), dma((18,)),
+            dma((6,)), dma((6,)), dma((18,)), dma((18,)),
             dma((4,)), dma((4,)), dma((6,)), dma((6,)), dma((6,)), dma((6,)), dma((1,)), dma((1,)),
-            dma((18,)), dma((18,)), dma((5,)), dma((5,)), dma((2,)), dma((2,)),
+            dma((18,)), dma((18,)), dma((6,)), dma((6,)), dma((2,)), dma((2,)),
         ],
         compiler_params=pltpu.CompilerParams(
             collective_id=0, has_side_effects=True, vmem_limit_bytes=62 << 20

time: 137 us -> 131 us (0.956); the launches traced: 134 us -> 131 us
  Pallas kernels: 134 us -> 130 us
    pallas_call x1, Pallas kernels: 132 us -> 128 us  [run_layer(): pl.pallas_call(layer_kernel, name='layer', out_shape=(block, block), in_s...]
where the time goes in v6:
time: 131 us
  Pallas kernels  130 us (99%)
    pallas_call x1, Pallas kernels, run_layer(): pl.pallas_call(layer_kernel, name='layer', out_shape=(block, block), in_s...  128 us

profile of v6, /device:TPU:3, one launch (start us, length us, event | category | flops | bytes accessed | tf_op | source)
XLA Modules:
  0.0 131.0 jit_solution(13976063075333227433)
XLA Ops:
  0.6 128.4 %layer.1 = (bf16[2,64,896]{2,1,0:T(8,128)(2,1)}, bf16[2,64,896]{2,1,0:T(8,128)(2,1)}) custom-call(s32[8,8]{1,0:T(8,128)} %bitcast.17, s32[8]{0:T(128)} %bitcast.18, s32[8]{0:T(128)} %bitcast.19, bf16[8,576,128]{2,1,0:T(8,128)(2,1)} %bitcast.13, bf16[8,576,1024]{2,1,0:T(8,128)(2,1)} %bitcast.10, bf16[16,512,128]{2,1,0:T(8,128)(2,1)} %up_ref.1, ...), custom_call_target="tpu_custom_call" | custom-call | flops 8220835840 | bytes 31457280 | tf_op jit(solution)/shard_map/layer/pallas_call | solution.py:594
  129.0 2.0 %finish.1 = (bf16[448,128]{1,0:T(8,128)(2,1)}, bf16[448,128]{1,0:T(8,128)(2,1)}) custom-call(bf16[2,64,896]{2,1,0:T(8,128)(2,1)} %get-tuple-element.6.att_ref, bf16[2,64,896]{2,1,0:T(8,128)(2,1)} %get-tuple-element.7.lay_ref), custom_call_target="tpu_custom_call" | custom-call | tf_op jit(solution)/shard_map/finish/pallas_call | solution.py:661

commit v7 on v6

--- a/solution.py
+++ b/solution.py
@@ -156,14 +156,10 @@
         arrived(block, r.at[4])
         push(buf.at[near(3), second], s, r, 13, ring(3))
 
-    def gather_step(buf, s, r, ways, i):
+    def gather_far(buf, s, r, ways, i):
         ring, peer, near, far = ways
         block = buf.at[far(0), upper]
         piece = buf.at[far(0), first]
-
-        @pl.when(i == 0)
-        def _():
-            arrived(block, r.at[5])
 
         @pl.when(i == 1)
         def _():
@@ -176,6 +172,18 @@
             push(buf.at[near(2), third], s, r, 16, peer)
             arrived(piece, r.at[10])
             push(buf.at[near(2), fourth], s, r, 17, peer)
+
+    def gather_ready(buf, r, ways, i):
+        far = ways[3]
+        block = buf.at[far(0), upper]
+        piece = buf.at[far(0), first]
+
+        @pl.when(i == 0)
+        def _():
+            arrived(block, r.at[5])
+
+        @pl.when(i == 1)
+        def _():
             arrived(block, r.at[9])
 
         @pl.when(i == 2)
@@ -193,16 +201,23 @@
 
     last = lax.rem(z + 2, 4)
 
-    def project(buf, w, s, r, out, landed, late_in, out_s, out_r):
-        gather_relay(buf, s, r, over_z)
+    def project(buf, parts, columns, w, s, r, out, landed, late_in, out_s, out_r):
+        for p, part in enumerate(parts):
+            gather_relay(part, s.at[p], r.at[p], over_z)
 
         def step(i, carry):
             zp = lax.rem(z + 4 - order(i), 4)
-            gather_step(buf, s, r, over_z, i)
-            left_rows = buf[pl.ds(2 * zp, 2)].reshape(2 * rows, buf.shape[2])
-            product = lax.dot_general(
-                left_rows, w[...], (((1,), (1,)), ((), ())), preferred_element_type=f32
-            )
+            for p, part in enumerate(parts):
+                gather_far(part, s.at[p], r.at[p], over_z, i)
+            product = 0.0
+            for p, part in enumerate(parts):
+                gather_ready(part, r.at[p], over_z, i)
+                start, width = columns[p]
+                left_rows = buf[pl.ds(2 * zp, 2), :, start : start + width]
+                product += lax.dot_general(
+                    left_rows.reshape(2 * rows, width), w[:, start : start + width],
+                    (((1,), (1,)), ((), ())), preferred_element_type=f32,
+                )
             out[pl.ds(2 * zp, 2)] = product.astype(bf16).reshape(2, rows, both)
 
             @pl.when((zp != x) & (i < 3))
@@ -350,15 +365,6 @@
 
     lax.fori_loop(0, GROUPS, widen, 0)
     count = GROUPS * slots
-    for h in range(heads):
-        head_rows = jnp.concatenate(
-            [wide[lane, pl.ds(h, count, stride=heads), :] for lane in range(KV // 128)], axis=1
-        )
-        vals[:, h * 128 : (h + 1) * 128] = jnp.dot(
-            head_rows.astype(jnp.bfloat16),
-            up_buf[h],
-            preferred_element_type=jnp.float32,
-        ).astype(jnp.bfloat16)
     row = lax.broadcasted_iota(jnp.int32, (count, count), 0)
     column = lax.broadcasted_iota(jnp.int32, (count, count), 1)
     source = row
@@ -367,10 +373,23 @@
         own_row = group * slots + slot_ref[group]
         source = jnp.where(row == own_row, partner * slots + slot_ref[partner], source)
     place = jnp.where(column == source, 1.0, 0.0).astype(jnp.bfloat16)
-    vb[q] = jnp.dot(place, vals[...], preferred_element_type=jnp.float32).astype(
-        jnp.bfloat16
-    )
-    gather_start(vb, v_s, v_r, over_z)
+    half_cols = heads * 64
+    v_parts = [vb.at[:, :, pl.ds(p * half_cols, half_cols)] for p in range(2)]
+    for p in range(2):
+        cols = slice(p * half_cols, (p + 1) * half_cols)
+        for h in range(p * heads // 2, (p + 1) * heads // 2):
+            head_rows = jnp.concatenate(
+                [wide[lane, pl.ds(h, count, stride=heads), :] for lane in range(KV // 128)], axis=1
+            )
+            vals[:, h * 128 : (h + 1) * 128] = jnp.dot(
+                head_rows.astype(jnp.bfloat16),
+                up_buf[h],
+                preferred_element_type=jnp.float32,
+            ).astype(jnp.bfloat16)
+        vb[q, :, cols] = jnp.dot(
+            place, vals[:, cols], preferred_element_type=jnp.float32
+        ).astype(jnp.bfloat16)
+        gather_start(v_parts[p], v_s.at[p], v_r.at[p], over_z)
 
     def weight_ready(i):
         src, dst = weights[i]
@@ -383,15 +402,15 @@
     turned[...] = resid_both[...].astype(f32)
     resid_rows[...] = jnp.transpose(turned[...], (1, 0))
     gain_row[...] = jnp.transpose(gain_both[...].astype(f32), (1, 0))[:1]
-    project(vb, wo, v_s, v_r, c_out, c_in, cl_in, c_s, c_r)
+    project(vb, v_parts, ((0, half_cols), (half_cols, half_cols)), wo, v_s, v_r, c_out, c_in, cl_in, c_s, c_r)
     attn = gathered_sum(c_out, c_in, cy_out, cy_in, c_s, c_r)
-    att_x[c] = attn.astype(bf16)
-    remote(att_x.at[c], att_x.at[c], o_s.at[0], o_r.at[0], sibling).start()
     resid = resid_rows[mine] + attn
     resid_rows[mine] = resid
     xb[g, :, :both] = (resid * gain_row[...]).astype(bf16)
     xb[g, :, both:] = with_sum(jnp.sum(resid * resid, axis=1, keepdims=True))
     gather_start(xb, x_s, x_r, over_x)
+    att_x[c] = attn.astype(bf16)
+    remote(att_x.at[c], att_x.at[c], o_s.at[0], o_r.at[0], sibling).start()
     for i in range(3, 6):
         weight_ready(i)
 
@@ -399,7 +418,8 @@
 
     def first_products(i, carry):
         xp = lax.rem(x + 4 - order(i), 4)
-        gather_step(xb, x_s, x_r, over_x, i)
+        gather_far(xb, x_s, x_r, over_x, i)
+        gather_ready(xb, x_r, over_x, i)
         block = xb[pl.ds(2 * xp, 2)].reshape(2 * rows, both + 128)
         pair = pl.ds(2 * xp, 2)
         lhs = block[:, :both]
@@ -488,10 +508,9 @@
             other_z(1 + 2 * j),
         ).start()
 
-    lax.fori_loop(0, 1, second_a, 0)
     for j in range(2):
         relay_b(j)
-    lax.fori_loop(1, 3, second_a, 0)
+    lax.fori_loop(0, 2, second_a, 0)
     for j in range(2):
         arrived(b_in.at[1 - j, j], b_r.at[2 + j])
         arrived(b_in.at[j, j], b_r.at[4 + j])
@@ -504,7 +523,7 @@
     b2_out[:, b_cols:] = with_sum(total_squares(away[:, b_cols:]))
     remote(b2_out, b2_in, b2_s.at[0], b2_r.at[0], y_peer).start()
     b_keep[...] = sum_b(yh)
-    lax.fori_loop(3, 4, second_a, 0)
+    lax.fori_loop(2, 4, second_a, 0)
     for j in range(2):
         relay_a(j)
     arrived(b2_in, b2_r.at[0])
@@ -521,7 +540,9 @@
             gate / (1.0 + jnp.exp(-gate)) * (upward * scale)
         ).astype(bf16)
 
+    h_parts = (hb.at[:, :, pl.ds(A_COLS, b_half)], hb.at[:, :, pl.ds(0, A_COLS)])
     write_hidden(A_COLS, sum_b2(0, b_half), sum_b2(b_half, b_half))
+    gather_start(h_parts[0], h_s.at[0], h_r.at[0], over_z)
     for j in range(2):
         arrived(a_in.at[1 - j, halves[j]], a_r.at[2 + j])
         arrived(a_in.at[j, halves[j]], a_r.at[4 + j])
@@ -534,8 +555,8 @@
         )
 
     write_hidden(0, sum_a(0), sum_a(A_COLS))
-    gather_start(hb, h_s, h_r, over_z)
-    project(hb, wd, h_s, h_r, g_out, g_in, gl_in, g_s, g_r)
+    gather_start(h_parts[1], h_s.at[1], h_r.at[1], over_z)
+    project(hb, h_parts, ((A_COLS, b_half), (0, A_COLS)), wd, h_s, h_r, g_out, g_in, gl_in, g_s, g_r)
     down = gathered_sum(g_out, g_in, gy_out, gy_in, g_s, g_r)
     lay_x[c] = (resid_rows[mine] + down).astype(bf16)
     remote(lay_x.at[c], lay_x.at[c], o_s.at[1], o_r.at[1], sibling).start()
@@ -546,8 +567,9 @@
         left(lat_in.at[0], l_s.at[k])
     for i, (src, dst) in enumerate(weights):
         left(src, w_s.at[i])
-    finish_gather(vb, v_s)
-    finish_gather(hb, h_s)
+    for p in range(2):
+        finish_gather(v_parts[p], v_s.at[p])
+        finish_gather(h_parts[p], h_s.at[p])
     finish_sends(c_out, cy_out, c_s)
     finish_sends(g_out, gy_out, g_s)
     finish_gather(xb, x_s)
@@ -641,10 +663,10 @@
             pltpu.VMEM((1, both), f32),
             pltpu.VMEM((both, total_rows), f32),
             dma((2, slots)), dma, dma, dma((8,)), dma((8,)),
-            dma((6,)), dma((6,)), dma((6,)), dma((18,)), dma((18,)),
+            dma((6,)), dma((6,)), dma((6,)), dma((2, 18)), dma((2, 18)),
             dma((6,)), dma((6,)), dma((18,)), dma((18,)),
             dma((4,)), dma((4,)), dma((6,)), dma((6,)), dma((6,)), dma((6,)), dma((1,)), dma((1,)),
-            dma((18,)), dma((18,)), dma((6,)), dma((6,)), dma((2,)), dma((2,)),
+            dma((2, 18)), dma((2, 18)), dma((6,)), dma((6,)), dma((2,)), dma((2,)),
         ],
         compiler_params=pltpu.CompilerParams(
             collective_id=0, has_side_effects=True, vmem_limit_bytes=62 << 20

time: 131 us -> 130 us (level)
  Pallas kernels: 130 us -> 128 us
    pallas_call x1, Pallas kernels: 128 us -> 126 us  [run_layer(): pl.pallas_call(layer_kernel, name='layer', out_shape=(block, block), in_s...]
where the time goes in v7:
time: 130 us; the launch traced here: 129 us
  Pallas kernels  128 us (98%)
    pallas_call x1, Pallas kernels, run_layer(): pl.pallas_call(layer_kernel, name='layer', out_shape=(block, block), in_s...  126 us

profile of v7, /device:TPU:3, one launch (start us, length us, event | category | flops | bytes accessed | tf_op | source)
XLA Modules:
  0.0 129.1 jit_solution(5192936867058908216)
XLA Ops:
  0.6 126.4 %layer.1 = (bf16[2,64,896]{2,1,0:T(8,128)(2,1)}, bf16[2,64,896]{2,1,0:T(8,128)(2,1)}) custom-call(s32[8,8]{1,0:T(8,128)} %bitcast.17, s32[8]{0:T(128)} %bitcast.18, s32[8]{0:T(128)} %bitcast.19, bf16[8,576,128]{2,1,0:T(8,128)(2,1)} %bitcast.13, bf16[8,576,1024]{2,1,0:T(8,128)(2,1)} %bitcast.10, bf16[16,512,128]{2,1,0:T(8,128)(2,1)} %up_ref.1, ...), custom_call_target="tpu_custom_call" | custom-call | flops 8220835840 | bytes 31457280 | tf_op jit(solution)/shard_map/layer/pallas_call | solution.py:616
  127.1 2.0 %finish.1 = (bf16[448,128]{1,0:T(8,128)(2,1)}, bf16[448,128]{1,0:T(8,128)(2,1)}) custom-call(bf16[2,64,896]{2,1,0:T(8,128)(2,1)} %get-tuple-element.6.att_ref, bf16[2,64,896]{2,1,0:T(8,128)(2,1)} %get-tuple-element.7.lay_ref), custom_call_target="tpu_custom_call" | custom-call | tf_op jit(solution)/shard_map/finish/pallas_call | solution.py:683

commit v8 on v7

--- a/solution.py
+++ b/solution.py
@@ -583,14 +583,23 @@
     left(lay_x.at[0], o_s.at[1])
 
 
-def finish_kernel(att_ref, lay_ref, attended_ref, out_ref, turned):
+def finish_kernel(att_ref, lay_ref, attended_ref, out_ref):
     feats = attended_ref.shape[0]
+    both = 2 * feats
+    width = pl.cdiv(feats, 128) * 128
     c = lax.rem(lax.axis_index("tp"), 2)
-    own = pl.ds(pl.multiple_of(c * feats, feats), feats)
     for exchange, target in ((att_ref, attended_ref), (lay_ref, out_ref)):
-        stacked = exchange[...].reshape(-1, 2 * feats).astype(jnp.float32)
-        turned[...] = jnp.transpose(stacked, (1, 0))
-        target[...] = turned[own].astype(target.dtype)
+        rows = 2 * exchange.shape[1]
+
+        @pl.when(c == 0)
+        def _():
+            block = exchange[:, :, :width].reshape(rows, width)
+            target[...] = jnp.transpose(block, (1, 0))[:feats]
+
+        @pl.when(c == 1)
+        def _():
+            block = exchange[:, :, both - width :].reshape(rows, width)
+            target[...] = jnp.transpose(block, (1, 0))[width - feats :]
 
 
 def run_layer(
@@ -686,7 +695,6 @@
         out_shape=(turned, turned),
         in_specs=[vmem, vmem],
         out_specs=(vmem, vmem),
-        scratch_shapes=[pltpu.VMEM((both, total_rows), f32)],
     )(att_x, lay_x)
     return jnp.swapaxes(attended, 0, 1), jnp.swapaxes(layer_out, 0, 1)
 

time: 130 us -> 130 us (level)
  no operation moved by 1% of the time
where the time goes in v8:
time: 130 us; the launch traced here: 129 us
  Pallas kernels  128 us (98%)
    pallas_call x1, Pallas kernels, run_layer(): pl.pallas_call(layer_kernel, name='layer', out_shape=(block, block), in_s...  126 us

profile of v8, /device:TPU:3, one launch (start us, length us, event | category | flops | bytes accessed | tf_op | source)
XLA Modules:
  0.0 129.0 jit_solution(16970914982447676226)
XLA Ops:
  0.6 126.4 %layer.1 = (bf16[2,64,896]{2,1,0:T(8,128)(2,1)}, bf16[2,64,896]{2,1,0:T(8,128)(2,1)}) custom-call(s32[8,8]{1,0:T(8,128)} %bitcast.17, s32[8]{0:T(128)} %bitcast.18, s32[8]{0:T(128)} %bitcast.19, bf16[8,576,128]{2,1,0:T(8,128)(2,1)} %bitcast.13, bf16[8,576,1024]{2,1,0:T(8,128)(2,1)} %bitcast.10, bf16[16,512,128]{2,1,0:T(8,128)(2,1)} %up_ref.1, ...), custom_call_target="tpu_custom_call" | custom-call | flops 8220835840 | bytes 31457280 | tf_op jit(solution)/shard_map/layer/pallas_call | solution.py:625
  127.1 1.9 %finish.1 = (bf16[448,128]{1,0:T(8,128)(2,1)}, bf16[448,128]{1,0:T(8,128)(2,1)}) custom-call(bf16[2,64,896]{2,1,0:T(8,128)(2,1)} %get-tuple-element.6.att_ref, bf16[2,64,896]{2,1,0:T(8,128)(2,1)} %get-tuple-element.7.lay_ref), custom_call_target="tpu_custom_call" | custom-call | tf_op jit(solution)/shard_map/finish/pallas_call | solution.py:692

commit v9 on v7

--- a/solution.py
+++ b/solution.py
@@ -416,6 +416,8 @@
 
     gather_relay(xb, x_s, x_r, over_x)
 
+    a_parts = (pl.ds(0, A_COLS), pl.ds(A_COLS, A_COLS))
+
     def first_products(i, carry):
         xp = lax.rem(x + 4 - order(i), 4)
         gather_far(xb, x_s, x_r, over_x, i)
@@ -429,11 +431,13 @@
                 lhs, w[:, start : start + width], preferred_element_type=f32
             ).astype(bf16).reshape(2, rows, width)
 
-        part_a[pair, :, :A_COLS] = product(wg, 0, A_COLS)
-        part_a[pair, :, A_COLS:] = product(wu, 0, A_COLS)
-        remote(
-            part_a.at[2 * xp + 1 - yh], a1_in.at[xp], a1_s.at[xp], a1_r.at[xp], y_peer
-        ).start()
+        for p, w in enumerate((wg, wu)):
+            cols = a_parts[p]
+            part_a[pair, :, cols] = product(w, 0, A_COLS)
+            remote(
+                part_a.at[2 * xp + 1 - yh, :, cols], a1_in.at[xp, :, cols], a1_s.at[p, xp],
+                a1_r.at[p, xp], y_peer,
+            ).start()
         part_b[pair, :, :b_half] = product(wg, A_COLS, b_half)
         part_b[pair, :, b_half:b_cols] = product(wu, A_COLS, b_half)
         part_b[pair, :, b_cols:] = block[:, both:].reshape(2, rows, 128)
@@ -462,8 +466,11 @@
 
     def second_a(i, carry):
         xp = lax.rem(x + 4 - order(i), 4)
-        arrived(a1_in.at[xp], a1_r.at[xp])
-        a2[xp] = (part_a[2 * xp + yh].astype(f32) + a1_in[xp].astype(f32)).astype(bf16)
+        for p, cols in enumerate(a_parts):
+            arrived(a1_in.at[xp, :, cols], a1_r.at[p, xp])
+            a2[xp, :, cols] = (
+                part_a[2 * xp + yh, :, cols].astype(f32) + a1_in[xp, :, cols].astype(f32)
+            ).astype(bf16)
         role = lax.rem(xp + 4 - z, 4)
 
         @pl.when(role == 2)
@@ -574,7 +581,8 @@
     finish_sends(g_out, gy_out, g_s)
     finish_gather(xb, x_s)
     for i in range(4):
-        left(part_a.at[0], a1_s.at[i])
+        for p, cols in enumerate(a_parts):
+            left(part_a.at[0, :, cols], a1_s.at[p, i])
     for i in range(6):
         left(part_b.at[0], b_s.at[i])
         left(a2.at[0, upper], a_s.at[i])
@@ -665,7 +673,7 @@
             dma((2, slots)), dma, dma, dma((8,)), dma((8,)),
             dma((6,)), dma((6,)), dma((6,)), dma((2, 18)), dma((2, 18)),
             dma((6,)), dma((6,)), dma((18,)), dma((18,)),
-            dma((4,)), dma((4,)), dma((6,)), dma((6,)), dma((6,)), dma((6,)), dma((1,)), dma((1,)),
+            dma((2, 4)), dma((2, 4)), dma((6,)), dma((6,)), dma((6,)), dma((6,)), dma((1,)), dma((1,)),
             dma((2, 18)), dma((2, 18)), dma((6,)), dma((6,)), dma((2,)), dma((2,)),
         ],
         compiler_params=pltpu.CompilerParams(

time: 130 us -> 130 us (level)
  no operation moved by 1% of the time
where the time goes in v9:
time: 130 us; the launch traced here: 129 us
  Pallas kernels  129 us (99%)
    pallas_call x1, Pallas kernels, run_layer(): pl.pallas_call(layer_kernel, name='layer', out_shape=(block, block), in_s...  127 us

profile of v9, /device:TPU:3, one launch (start us, length us, event | category | flops | bytes accessed | tf_op | source)
XLA Modules:
  0.0 129.3 jit_solution(14675927146017271931)
XLA Ops:
  0.6 126.7 %layer.1 = (bf16[2,64,896]{2,1,0:T(8,128)(2,1)}, bf16[2,64,896]{2,1,0:T(8,128)(2,1)}) custom-call(s32[8,8]{1,0:T(8,128)} %bitcast.17, s32[8]{0:T(128)} %bitcast.18, s32[8]{0:T(128)} %bitcast.19, bf16[8,576,128]{2,1,0:T(8,128)(2,1)} %bitcast.13, bf16[8,576,1024]{2,1,0:T(8,128)(2,1)} %bitcast.10, bf16[16,512,128]{2,1,0:T(8,128)(2,1)} %up_ref.1, ...), custom_call_target="tpu_custom_call" | custom-call | flops 8220835840 | bytes 31457280 | tf_op jit(solution)/shard_map/layer/pallas_call | solution.py:624
  127.3 2.0 %finish.1 = (bf16[448,128]{1,0:T(8,128)(2,1)}, bf16[448,128]{1,0:T(8,128)(2,1)}) custom-call(bf16[2,64,896]{2,1,0:T(8,128)(2,1)} %get-tuple-element.6.att_ref, bf16[2,64,896]{2,1,0:T(8,128)(2,1)} %get-tuple-element.7.lay_ref), custom_call_target="tpu_custom_call" | custom-call | tf_op jit(solution)/shard_map/finish/pallas_call | solution.py:691
